TPU v7x, 128 devices: a whole 4x4x4 slice. The times are simulated.
128 devices in a mesh: src: 4 (over x), grp: 32 (over z, y, core).
Axes of the slice: x: 4, y: 4, z: 4, core: 2. Of those that a mesh axis runs over, the one named last changes fastest.
Arguments:
- source_points: bfloat16 [32768, 64], P('src'), may hold values from -6 to 6
- source_logmass: float32 [32768], P('src'), may hold values from -1 to 1
- target_points: bfloat16 [524288, 64], P(('src', 'grp')), may hold values from -1.796875 to 1.796875
- target_logmass: float32 [524288], P(('src', 'grp')), may hold values from -1 to 1
- target_potential: float32 [524288], P(('src', 'grp')), may hold values from -1.5 to 61.5
- tile_slot: int32 [256, 256], P('src', 'grp'), may hold values from 0 to 31, as said below
- tile_counts: int32 [256, 32], P('src', 'grp'), may hold values from 2 to 8
- fetch_ids: int32 [16, 256], P('src', 'grp'), may hold values from 0 to 31, as said below
Outputs:
- source_field: float32 [32768], P('src')
- target_field: float32 [524288], P(('src', 'grp'))
Inputs may be any that keep to these rules, and one draw needn't show every extreme that they name: `tile_slot`: within one source block and group the live slots name distinct entries; every entry 0 to 31 of a device's fetch list is named by some live slot of that device. `fetch_ids`: each device names 8 distinct blocks of each peer in its group; every target block is named by some device of its group.
All inputs are finite; a program needn't handle non-finite values.
Results may differ from a plain program's by a relative error of at most 0.0003.
Values may be sent and summed in bfloat16 or wider, within the bound.
No kernel may reach another device: no remote copies, remote signals or barrier semaphores. Data moves between devices by JAX's collectives and lax.ppermute only.
A program may use at most 64 MiB of HBM per device.

v0:
```python
import functools

import jax
import jax.numpy as jnp
from jax import lax
from jax.experimental import pallas as pl
from jax.experimental.pallas import tpu as pltpu
from jax.sharding import PartitionSpec as P

D = 64
BLOCK = 128
KG = 8
ITERS = 3
EPSILON = 0.25
LOWEST = -1e30
LOG2E = 1.4426950408889634
SCALE = LOG2E / EPSILON
PAIRS = 64
TAIL = 16
COPIES = 2
GROUP = 32
CAP = 8
EXTRA = 6
LEFT, RIGHT = 0, 1
FIRST, ROWS, COLUMNS = 0, 1, 2
PARTS = 4
LONG = 1024 * 1024
HEAD = 8
STRIDE = 64


SMEM = pl.BlockSpec(memory_space=pltpu.SMEM)
VMEM = pl.BlockSpec(memory_space=pltpu.VMEM)
HBM = pl.BlockSpec(memory_space=pltpu.HBM)
MIB = 1024 * 1024
PREPARE = pltpu.CompilerParams(vmem_limit_bytes=64 * MIB)
PASS = pltpu.CompilerParams(vmem_limit_bytes=53 * MIB)


def shape(dims, dtype=jnp.float32):
    return jax.ShapeDtypeStruct(dims, dtype)


def start_copies(pairs, sems):
    copies = [pltpu.make_async_copy(src, dst, sems.at[k]) for k, (src, dst) in enumerate(pairs)]
    for copy in copies:
        copy.start()
    return copies


def close_list(ref, hbm, pairs, last, none, sems):
    right = HEAD + (ref.shape[0] - HEAD) // 3
    tails = (pairs + TAIL - 1) // TAIL
    ref[0] = tails // (PAIRS // TAIL)
    ref[1] = tails % (PAIRS // TAIL)

    def pad(k, carry):
        ref[HEAD + pairs + k] = last
        ref[right + 2 * (pairs + k)] = none
        ref[right + 2 * (pairs + k) + 1] = none
        return carry

    lax.fori_loop(0, tails * TAIL - pairs, pad, 0)
    copy = pltpu.make_async_copy(ref, hbm.at[pl.ds(0, ref.shape[0])], sems.at[0])
    copy.start()
    return copy


def columns_kernel(half_ref, *refs):
    remotes, hbm, (*tables, ref, sems) = refs[:4], refs[4], refs[5:]
    for copy in start_copies(list(zip(remotes, tables)), sems):
        copy.wait()
    halves = tables[0].shape[1] // 2
    first = half_ref[0] * halves
    right = HEAD + (ref.shape[0] - HEAD) // 3

    def one_block(b, position):
        at = right + 2 * position
        tiles = jnp.int32(0)
        for group, (slots_ref, counts_ref) in enumerate((tables[0:2], tables[2:4])):
            for k in range(KG):
                ref[at + tiles + k] = slots_ref[k, first + b] + group * GROUP
            tiles = tiles + counts_ref[0, first + b]
        ref[at + tiles] = 2 * GROUP
        for k in range(KG):
            ref[HEAD + position + k] = b
        return position + (tiles + 1) // 2

    pairs = lax.fori_loop(0, halves, one_block, jnp.int32(0))
    close_list(ref, hbm, pairs, halves - 1, 2 * GROUP, sems).wait()


def same_targets(ids, rows, same_ref):
    peers, per_peer = ids[0].shape
    lane = lax.broadcasted_iota(jnp.int32, (1, BLOCK), 1)
    known = jnp.zeros((1, BLOCK), jnp.int32)
    for d in range(peers):
        for p in range(peers):
            for c in range(per_peer):
                known = jnp.where(lane == (d * peers + p) * per_peer + c, ids[d][p, c], known)
    for p in range(peers):
        for c in range(per_peer):
            q = p * per_peer + c
            same = jnp.logical_and(known == ids[0][p, c], lane // per_peer % peers == p)
            for d in range(peers):
                own = jnp.logical_and(same, lane // GROUP == d)
                rows[pl.ds(d * GROUP + q, 1), :] = jnp.where(own, 1.0, 0.0)
    same_ref[...] = rows[...].astype(jnp.bfloat16)


def rows_kernel(half_ref, *refs):
    remotes, hbm, locals_ = refs[:4], refs[4], refs[5:]
    *tables, ref, lists, sizes, sems = locals_
    copies = start_copies(list(zip(remotes, tables)), sems)
    groups = (tables[0:2], tables[2:4])
    halves = tables[0].shape[1] // 2
    slots = 2 * GROUP
    first = half_ref[0] * halves
    right = HEAD + (ref.shape[0] - HEAD) // 3

    def clear(q, carry):
        sizes[q] = 0
        return carry

    lax.fori_loop(0, slots + 1, clear, 0, unroll=13)
    for copy in copies:
        copy.wait()

    def one_block(b, carry):
        def append(named):
            known = [sizes[slot] for slot in named]
            for slot, size in zip(named, known):
                lists[slot * STRIDE + size] = b
            for slot, size in zip(named, known):
                sizes[slot] = size + 1

        append([table[k, first + b] + group * GROUP for group, (table, _) in enumerate(groups) for k in range(2)])
        for group, (table, counts_ref) in enumerate(groups):
            count = counts_ref[0, first + b]

            def more(table=table, group=group, count=count):
                append(
                    [jnp.where(k < count, table[k, first + b] + group * GROUP, slots) for k in range(2, KG)]
                )

            pl.when(count > 2)(more)
        return carry

    lax.fori_loop(0, halves, one_block, 0)
    batch = 4

    def one_pair(q, position, k):
        ref[HEAD + position + k] = q
        for j in range(2):
            ref[right + 2 * (position + k) + j] = lists[q * STRIDE + 2 * k + j]

    def some_slots(t, position):
        counted = [sizes[t * batch + j] for j in range(batch)]
        for j, size in enumerate(counted):
            lists[(t * batch + j) * STRIDE + size] = halves
        counted = [(size + 1) // 2 for size in counted]
        places = [position]
        for pairs in counted:
            places.append(places[-1] + pairs)
        for j in range(batch):
            for k in range(3):
                one_pair(t * batch + j, places[j], k)

        def rest():
            for j in range(batch):

                def another(k, carry, j=j):
                    one_pair(t * batch + j, places[j], k)
                    return carry

                lax.fori_loop(3, counted[j], another, 0)

        pl.when(functools.reduce(jnp.maximum, counted) > 3)(rest)
        return places[-1]

    pairs = lax.fori_loop(0, slots // batch, some_slots, jnp.int32(0))
    close_list(ref, hbm, pairs, slots - 1, halves, sems).wait()


def list_shape(halves):
    room = HEAD + 3 * (halves * KG + 2 * GROUP + PAIRS + KG)
    return ((room + 1023) // 1024 * 1024,)


def make_list(kernel, half, remotes):
    own = [pltpu.SMEM(value.shape, value.dtype) for value in remotes]
    own.append(pltpu.SMEM(list_shape(remotes[0].shape[1] // 2), jnp.int32))
    if kernel is rows_kernel:
        own.append(pltpu.SMEM(((2 * GROUP + 1) * STRIDE,), jnp.int32))
        own.append(pltpu.SMEM((2 * GROUP + 1,), jnp.int32))
    return pl.pallas_call(
        kernel,
        out_shape=shape((LONG,), jnp.int32),
        in_specs=[SMEM] + [HBM] * len(remotes),
        out_specs=HBM,
        scratch_shapes=[*own, pltpu.SemaphoreType.DMA((len(remotes),))],
        compiler_params=PREPARE,
    )(half.reshape(1), *remotes)


def split3(values):
    high = values.astype(jnp.bfloat16)
    rest = values - high.astype(jnp.float32)
    middle = rest.astype(jnp.bfloat16)
    low = (rest - middle.astype(jnp.float32)).astype(jnp.bfloat16)
    return high, middle, low


def whole(parts):
    high, middle, low = [part.astype(jnp.float32) for part in parts]
    return high + middle + low


def log_sum(values):
    top = functools.reduce(jnp.maximum, values)
    return top + jnp.log2(sum(jnp.exp2(value - top) for value in values))


def pack_kernel(place_ref, *refs):
    count = (len(refs) - 3) // 2
    remotes, (out_ref, norm_ref, *locals_, sems) = refs[:count], refs[count:]
    *ids_refs, points, potential, logmass = locals_
    copies = start_copies(list(zip(remotes, locals_)), sems)
    place = place_ref[0]
    peers, per_peer = ids_refs[0].shape
    for copy in copies:
        copy.wait()

    def one_norm(t, carry):
        wide = points[:, pl.ds(pl.multiple_of(t * BLOCK, BLOCK), BLOCK)].astype(jnp.float32)
        norm_ref[pl.ds(t, 1), :] = 0.5 * jnp.sum(wide * wide, axis=0, keepdims=True)
        return carry

    lax.fori_loop(0, norm_ref.shape[0], one_norm, 0, unroll=8)
    for d, ids_ref in enumerate(ids_refs):
        other = lax.rem(place - d + peers, peers)
        rows = []
        for c in range(per_peer):
            t = ids_ref[place, c]
            block = points[:, pl.ds(pl.multiple_of(t * BLOCK, BLOCK), BLOCK)]
            start = SCALE * (potential[pl.ds(t, 1), :] - norm_ref[pl.ds(t, 1), :])
            mass = LOG2E * logmass[pl.ds(t, 1), :]
            rows += [part.astype(jnp.float32) for part in split3(start) + split3(mass)]
            out_ref[other, c * D : (c + 1) * D, :] = block
        out_ref[other, per_peer * D :, :] = jnp.concatenate(rows, axis=0).astype(jnp.bfloat16)


def pack(place, ids, *values):
    remotes = [*ids, *values]
    return pl.pallas_call(
        pack_kernel,
        out_shape=[shape((len(ids), CAP * (D + EXTRA), BLOCK), jnp.bfloat16), shape(values[1].shape)],
        in_specs=[SMEM] + [HBM] * len(remotes),
        out_specs=[VMEM, VMEM],
        scratch_shapes=[pltpu.SMEM(value.shape, value.dtype) for value in ids]
        + [pltpu.VMEM(value.shape, value.dtype) for value in values]
        + [pltpu.SemaphoreType.DMA((len(remotes),))],
        compiler_params=PREPARE,
    )(place.reshape(1), *remotes)


def merge_kernel(peers, place_ref, *refs):
    sums, ids, (logmass_ref, norm_ref, out_ref, parts) = refs[:peers], refs[peers : 2 * peers], refs[2 * peers :]
    place = place_ref[0]
    parts[...] = jnp.full_like(parts, LOWEST)
    for d in range(peers):
        for c in range(sums[d].shape[0]):
            parts[d, pl.ds(ids[d][place, c], 1), :] = sums[d][c : c + 1, :]
    merged = log_sum([parts[d] for d in range(peers)])
    out_ref[...] = (LOG2E * logmass_ref[...] - merged) * (1.0 / SCALE) + norm_ref[...]


def merge(place, sums, ids, logmass, norm):
    peers = len(ids)
    return pl.pallas_call(
        functools.partial(merge_kernel, peers),
        out_shape=shape(norm.shape),
        in_specs=[SMEM] + [VMEM] * peers + [SMEM] * peers + [VMEM] * 2,
        out_specs=VMEM,
        scratch_shapes=[pltpu.VMEM((peers, *norm.shape), jnp.float32)],
        compiler_params=PASS,
    )(place.reshape(1), *sums, *ids, logmass, norm)


def scaled_block(points, b):
    wide = points[:, pl.ds(pl.multiple_of(b * BLOCK, BLOCK), BLOCK)].astype(jnp.float32)
    scaled = SCALE * wide
    high = scaled.astype(jnp.bfloat16)
    low = (scaled - high.astype(jnp.float32)).astype(jnp.bfloat16)
    return wide, jnp.concatenate([high, low], axis=0)


def source_kernel(half_ref, points_hbm, logmass_hbm, *refs):
    count = (len(refs) - 8) // 2
    ids_hbm, (blocks_hbm, norm_ref, same_ref, points, logmass, blocks, rows, *ids, sems) = refs[:count], refs[count:]
    halves = blocks.shape[1] - 1
    own = pl.ds(pl.multiple_of(half_ref[0] * halves, halves), halves)
    at = pl.multiple_of(half_ref[0] * (halves * BLOCK), halves * BLOCK)
    pairs = [(points_hbm.at[:, pl.ds(at, halves * BLOCK)], points), (logmass_hbm.at[own], logmass)]
    for copy in start_copies(pairs + list(zip(ids_hbm, ids)), sems):
        copy.wait()
    parts = split3(LOG2E * logmass[...])
    blocks[LEFT, halves] = jnp.concatenate([*parts, jnp.zeros_like(parts[0])], axis=0)
    blocks[RIGHT, halves] = jnp.zeros((BLOCK, BLOCK), jnp.bfloat16)

    part = halves // PARTS

    def one_block(b, carry):
        wide, both = scaled_block(points, b)
        norm_ref[pl.ds(b, 1), :] = 0.5 * jnp.sum(wide * wide, axis=0, keepdims=True)
        blocks[RIGHT, b] = both
        blocks[LEFT, b] = both.T
        return carry

    copies = []
    for k in range(PARTS):
        lax.fori_loop(k * part, (k + 1) * part, one_block, 0, unroll=4)
        own = (slice(None), pl.ds(k * part, part + (k == PARTS - 1)))
        copies.append(pltpu.make_async_copy(blocks.at[own], blocks_hbm.at[own], sems.at[2 + count + k]))
        copies[-1].start()
    same_targets(ids, rows, same_ref)
    for copy in copies:
        copy.wait()


def source(half, halves, points, logmass, ids):
    blocks = (2, halves + 1, BLOCK, BLOCK)
    return pl.pallas_call(
        source_kernel,
        out_shape=[
            shape(blocks, jnp.bfloat16),
            shape((halves, BLOCK)),
            shape((BLOCK, BLOCK), jnp.bfloat16),
        ],
        in_specs=[SMEM] + [HBM] * (2 + len(ids)),
        out_specs=[HBM, VMEM, VMEM],
        scratch_shapes=[
            pltpu.VMEM((D, halves * BLOCK), jnp.bfloat16),
            pltpu.VMEM((halves, BLOCK), jnp.float32),
            pltpu.VMEM(blocks, jnp.bfloat16),
            pltpu.VMEM((BLOCK, BLOCK), jnp.float32),
        ]
        + [pltpu.SMEM(value.shape, value.dtype) for value in ids]
        + [pltpu.SemaphoreType.DMA((2 + len(ids) + PARTS,))],
        compiler_params=PASS,
    )(half.reshape(1), points, logmass, *ids)


def field_bias(mass_ref, parts_ref):
    rows = parts_ref.shape[1]
    mass = whole([mass_ref[k * rows : (k + 1) * rows, :] for k in range(3)])
    return mass - log_sum([parts_ref[k] for k in range(parts_ref.shape[0])])


def potential_bias(mass_ref, chosen_refs, *refs):
    dot = functools.partial(jnp.dot, preferred_element_type=jnp.float32)
    mass = whole([mass_ref[0, : 2 * GROUP, :], mass_ref[0, 2 * GROUP :, :], mass_ref[1, : 2 * GROUP, :]])
    out = []
    for group in range(2):
        own = slice(group * GROUP, (group + 1) * GROUP)
        chosen = chosen_refs[group][...]
        sums = jnp.concatenate([ref[own, :] for ref in refs], axis=0)
        parts = sum(dot(chosen, part) for part in split3(sums))
        known = dot(chosen, jnp.ones_like(chosen)) > 0.5
        parts = jnp.where(known, parts, LOWEST)
        merged = log_sum([parts[k * GROUP : (k + 1) * GROUP] for k in range(len(refs))])
        out.append(mass[own, :] - merged)
    return jnp.concatenate(out, axis=0)


def unpack(raw, left, start_ref, mass_ref, first, stop):
    def one_peer(peer, carry):
        rows = raw[peer, CAP * D :, :].astype(jnp.float32)
        for c in range(CAP):
            q = peer * CAP + c
            block = raw[peer, c * D : (c + 1) * D, :]
            left[q] = jnp.concatenate([block, block], axis=0).T
            high, middle, low, *mass = [rows[EXTRA * c + k : EXTRA * c + k + 1] for k in range(EXTRA)]
            start_ref[pl.ds(q, 1), :] = high + middle + low
            mass_ref[pl.ds(q, 1), :] = mass[0] + mass[1] + mass[2]
        return carry

    lax.fori_loop(first, stop, one_peer, 0)


def pass_kernel(kind, *refs):
    columns, peaks, masses, list_ref, left_ref, right_ref, sems = refs[-7:]
    lefts, rights = columns.shape[0], peaks.shape[1] - 1
    peers = GROUP // CAP
    part = lefts // PARTS
    left_parts = []
    if kind == FIRST:
        list_hbm, near_hbm, far_hbm, points_hbm, half_ref = refs[:5]
        out_ref, left_hbm, mass_ref, bias_ref, raw, points = refs[5:-7]
        own = rights * BLOCK
        at = pl.multiple_of(half_ref[0] * own, own)
        early = [(near_hbm, raw.at[pl.ds(0, peers)]), (far_hbm, raw.at[pl.ds(peers, peers)])]
        early.insert(0, (points_hbm.at[:, pl.ds(at, own)], points))
        late = []
    elif kind == ROWS:
        list_hbm, left_hbm, points_hbm = refs[:3]
        *col_parts, near_same, far_same, out_ref, bias_ref, mass = refs[3:-7]
        early = [(left_hbm.at[pl.ds(lefts, 2)], mass)]
        late = [(points_hbm.at[RIGHT, pl.ds(0, rights)], right_ref)]
        left_parts = [left_hbm.at[pl.ds(k * part, part)] for k in range(PARTS)]
    else:
        list_hbm, near_hbm, far_hbm, points_hbm, rows_ref, out_ref, bias_ref, mass = refs[:-7]
        early = [(points_hbm.at[LEFT, lefts], mass)]
        late = [
            (raw_hbm.at[:, pl.ds(0, CAP * D)], right_ref.at[pl.ds(group * peers, peers)])
            for group, raw_hbm in enumerate((near_hbm, far_hbm))
        ]
        left_parts = [points_hbm.at[LEFT, pl.ds(k * part, part)] for k in range(PARTS)]
    late.append((list_hbm.at[pl.ds(0, list_ref.shape[0])], list_ref))
    pairs = early + late + [(ref, left_ref.at[pl.ds(k * part, part)]) for k, ref in enumerate(left_parts)]
    copies = start_copies(pairs, sems)
    peaks[...] = jnp.full_like(peaks, LOWEST)
    masses[...] = jnp.zeros_like(masses)
    if kind == FIRST:
        copies[0].wait()

        def scale(b, carry):
            right_ref[b] = scaled_block(points, b)[1]
            return carry

        lax.fori_loop(0, rights, scale, 0, unroll=8)
        for group in range(2):
            copies[1 + group].wait()
            unpack(raw, left_ref, bias_ref, mass_ref, group * peers, (group + 1) * peers)
        high, middle, low = split3(mass_ref[...])
        left_ref[lefts] = jnp.concatenate([high, middle], axis=0)
        left_ref[lefts + 1] = jnp.concatenate([low, jnp.zeros_like(low)], axis=0)
        hand_on = pltpu.make_async_copy(left_ref, left_hbm, sems.at[len(pairs)])
        hand_on.start()
    else:
        for copy in copies[: len(early)]:
            copy.wait()
    if kind == ROWS:
        bias_ref[...] = potential_bias(mass, (near_same, far_same), *col_parts)
    elif kind == COLUMNS:
        bias_ref[...] = field_bias(mass, rows_ref)
    square = (BLOCK, BLOCK)
    lane = lax.broadcasted_iota(jnp.int32, square, 1)
    eye = jnp.where(lane == lax.broadcasted_iota(jnp.int32, square, 0), 1.0, 0.0).astype(jnp.bfloat16)
    lane = jnp.where(lane < 3 * GROUP, lane % GROUP, -1)
    for group in range(lefts // GROUP):
        high, middle, low = split3(bias_ref[group * GROUP : (group + 1) * GROUP, :])
        parts = jnp.concatenate([high, middle, low, jnp.zeros_like(high)], axis=0)
        turned = lax.dot_general(
            eye, parts, (((1,), (1,)), ((), ())), preferred_element_type=jnp.float32
        )

        def fill(k, carry, group=group, turned=turned):
            columns[group * GROUP + k] = jnp.where(lane == k, turned, 0.0).astype(jnp.bfloat16)
            return carry

        lax.fori_loop(0, GROUP, fill, 0, unroll=4)
    for copy in copies[len(early) : len(early) + len(late)]:
        copy.wait()
    rights_at = HEAD + (list_ref.shape[0] - HEAD) // 3
    ones = jnp.ones((BLOCK, 2 * BLOCK), jnp.bfloat16)

    def fold(copy, r, scores):
        scores = scores.reshape(BLOCK // 8, 8, BLOCK)
        old = peaks[copy, r]
        top = jnp.maximum(old, jnp.max(scores, axis=0))
        mass = jnp.sum(jnp.exp2(scores - top[None]), axis=0)
        masses[copy, r] = masses[copy, r] * jnp.exp2(old - top) + mass
        peaks[copy, r] = top

    def right_block(r):
        r = jnp.minimum(r, rights - 1)
        if kind != COLUMNS:
            return right_ref[r]
        block = right_ref[r // CAP, pl.ds(pl.multiple_of(r % CAP * D, D), D), :]
        return jnp.concatenate([block, block], axis=0)

    def wait_for(known, needed):
        if not left_parts:
            return known

        def wait(k, carry):
            at = pl.ds(k * part, part)
            source = left_hbm.at[at] if kind == ROWS else points_hbm.at[LEFT, at]
            pltpu.make_async_copy(source, left_ref.at[at], sems.at[len(early) + len(late) + k]).wait()
            return carry

        lax.fori_loop(known, needed, wait, 0)
        return jnp.maximum(known, needed)

    def step(start, count, t, known):
        known = wait_for(known, list_ref[HEAD + start + t * count + count - 1] // part + 1)
        for u in range(count):
            i = start + t * count + u
            l = list_ref[HEAD + i]
            first, second = list_ref[rights_at + 2 * i], list_ref[rights_at + 2 * i + 1]
            left = jnp.concatenate([left_ref[l], columns[l]], axis=1)
            right = jnp.concatenate([right_block(first), right_block(second)], axis=1)
            scores = jnp.dot(
                left, jnp.concatenate([right, ones], axis=0), preferred_element_type=jnp.float32
            )
            fold((2 * u) % COPIES, first, scores[:, :BLOCK])
            fold((2 * u + 1) % COPIES, second, scores[:, BLOCK:])
        return known

    known = lax.fori_loop(0, list_ref[0], functools.partial(step, 0, PAIRS), jnp.int32(0))
    known = lax.fori_loop(0, list_ref[1], functools.partial(step, list_ref[0] * PAIRS, TAIL), known)
    wait_for(known, PARTS)

    def finish(octet, carry):
        rows = []
        for k in range(8):
            r = octet * 8 + k
            tops = [peaks[copy, r] for copy in range(COPIES)]
            top = jnp.max(functools.reduce(jnp.maximum, tops), axis=0, keepdims=True)
            mass = sum(masses[copy, r] * jnp.exp2(tops[copy] - top) for copy in range(COPIES))
            rows.append(top + jnp.log2(jnp.sum(mass, axis=0, keepdims=True)))
        out_ref[0, pl.ds(pl.multiple_of(octet * 8, 8), 8), :] = jnp.concatenate(rows, axis=0)
        return carry

    lax.fori_loop(0, rights // 8, finish, 0)
    for k in range(1, out_ref.shape[0]):
        out_ref[k] = out_ref[0]
    if kind == FIRST:
        hand_on.wait()


def log_sums(kind, pairs, halves, remotes, parts, copies, keep=False):
    slots = 2 * GROUP
    lefts, rights = (halves, slots) if kind == COLUMNS else (slots, halves)
    form = (2 * GROUP // CAP, CAP * D, BLOCK) if kind == COLUMNS else (rights, BLOCK, BLOCK)
    held = lefts
    outs, bias = [shape((copies, rights, BLOCK))], pltpu.VMEM((lefts, BLOCK), jnp.float32)
    if kind == FIRST:
        held = lefts + 2
        outs.append(shape((held, BLOCK, BLOCK), jnp.bfloat16))
        scratch = [bias, bias, pltpu.VMEM((2 * GROUP // CAP, CAP * (D + EXTRA), BLOCK), jnp.bfloat16)]
        scratch.append(pltpu.VMEM((D, halves * BLOCK), jnp.bfloat16))
    elif kind == ROWS:
        scratch = [bias, pltpu.VMEM((2, BLOCK, BLOCK), jnp.bfloat16)]
    else:
        scratch = [pltpu.VMEM((BLOCK, BLOCK), jnp.bfloat16)]
        if keep:
            outs.append(shape((lefts, BLOCK)))
        else:
            scratch.insert(0, bias)
    return pl.pallas_call(
        functools.partial(pass_kernel, kind),
        out_shape=outs,
        in_specs=[HBM] * (1 + len(remotes)) + [SMEM if kind == FIRST else VMEM] * len(parts),
        out_specs=[VMEM, HBM] if kind == FIRST else [VMEM] * len(outs),
        scratch_shapes=scratch
        + [
            pltpu.VMEM((lefts, BLOCK, BLOCK), jnp.bfloat16),
            pltpu.VMEM((COPIES, rights + 1, 8, BLOCK), jnp.float32),
            pltpu.VMEM((COPIES, rights + 1, 8, BLOCK), jnp.float32),
            pltpu.SMEM(list_shape(halves), jnp.int32),
            pltpu.VMEM((held, BLOCK, BLOCK), jnp.bfloat16),
            pltpu.VMEM(form, jnp.bfloat16),
            pltpu.SemaphoreType.DMA((5 + PARTS,)),
        ],
        compiler_params=PREPARE if kind == FIRST else PASS,
    )(pairs, *remotes, *parts)


def ring(values, axis, size, stride=1):
    places = lax.axis_size(axis)
    out = [values]
    for d in range(1, size):
        pairs = []
        for i in range(places):
            place = i // stride % size
            pairs.append((i, i + ((place + d) % size - place) * stride))
        out.append(lax.ppermute(values, axis, pairs))
    return out


def shards(
    source_points,
    source_logmass,
    target_points,
    target_logmass,
    target_potential,
    tile_slot,
    tile_counts,
    fetch_ids,
):
    peers = lax.axis_size("src")
    blocks = tile_counts.shape[0]
    halves = blocks // 2
    per_peer = fetch_ids.shape[1]
    owned = target_potential.shape[0] // BLOCK
    count = peers * per_peer
    place = lax.axis_index("src")
    half = lax.axis_index("grp") % 2

    def swap(values):
        return ring(values, "grp", 2, 1)[1]

    tiles = [tile_slot.T, tile_counts.T]
    ids = ring(fetch_ids, "src", peers)
    ids, tiles = lax.optimization_barrier((ids, tiles + [swap(part) for part in tiles]))
    packed, target_half = pack(
        place,
        ids,
        target_points.T,
        target_potential.reshape(owned, BLOCK),
        target_logmass.reshape(owned, BLOCK),
    )
    row_pairs = make_list(rows_kernel, half, tiles)
    fetched = lax.all_to_all(packed, "src", split_axis=0, concat_axis=0, tiled=True)
    fetched, row_pairs, ids, tiles = lax.optimization_barrier((fetched, row_pairs, ids, tiles))
    col_pairs = make_list(columns_kernel, half, tiles)
    *both, col_pairs = lax.optimization_barrier((fetched, swap(fetched), col_pairs))

    groups = lax.axis_size("grp")
    same_core = [list(range(core, groups, 2)) for core in range(2)]
    for sweep_index in range(ITERS):
        if sweep_index == 0:
            turned = source_points.T
            rows, targets = log_sums(FIRST, row_pairs, halves, [*both, turned], [half.reshape(1)], groups // 2)
            rows, turned, logmass, ids = lax.optimization_barrier((rows, turned, source_logmass, ids))
            points, source_half, same = source(half, halves, turned, logmass.reshape(blocks, BLOCK), ids)
            same = [same, swap(same)]
        else:
            (rows,) = log_sums(ROWS, row_pairs, halves, [targets, points], col_parts + same, groups // 2)
        rows = lax.all_to_all(
            rows, "grp", split_axis=0, concat_axis=0, tiled=True, axis_index_groups=same_core
        )
        last = sweep_index == ITERS - 1
        cols, *fields = log_sums(COLUMNS, col_pairs, halves, [*both, points], [rows], 1, keep=last)
        cols = cols[0]
        if sweep_index < ITERS - 1:
            other = swap(cols)
            cols = log_sum([cols, jnp.concatenate([other[count:], other[:count]], axis=0)])
            col_parts = ring(cols, "src", peers)
    field, half = lax.optimization_barrier((fields[0], half))
    field = field * (1.0 / SCALE) + source_half
    low = half == 0
    other = swap(field)
    source_field = jnp.concatenate([jnp.where(low, field, other), jnp.where(low, other, field)], axis=0)

    cols = log_sum([cols[:count], swap(cols[count:])]).reshape(peers, per_peer, BLOCK)
    cols, last_place, ids, target_half, target_logmass = lax.optimization_barrier(
        (cols, place, ids, target_half, target_logmass)
    )
    back = []
    for d in range(peers):
        wanted = lax.dynamic_slice(cols, ((last_place + d) % peers, 0, 0), (1, per_peer, BLOCK))[0]
        pairs = [(i, (i + d) % peers) for i in range(peers)]
        back.append(wanted if d == 0 else lax.ppermute(wanted, "src", pairs))
    target_field = merge(last_place, back, ids, target_logmass.reshape(owned, BLOCK), target_half).reshape(-1)
    return (source_field.reshape(-1), target_field)


def solution(mesh):
    return jax.shard_map(
        shards,
        mesh=mesh,
        in_specs=(
            P("src", None),
            P("src"),
            P(("src", "grp"), None),
            P(("src", "grp")),
            P(("src", "grp")),
            P("src", "grp"),
            P("src", "grp"),
            P("src", "grp"),
        ),
        out_specs=(P("src"), P(("src", "grp"))),
        check_vma=False,
    )
```

profile of v0, /device:TPU:0, one launch (start us, length us, event | category | flops | bytes accessed | tf_op | source)
XLA Modules:
  0.0 132.5 jit_solution(1523869778352920714)
XLA Ops:
  0.6 0.1 collective-permute-start.3
  0.7 3.2 %collective-permute-start.1 = (s32[4,8]{1,0:T(4,128)}, s32[4,8]{1,0:T(4,128)}, u32[]{:S(2)}, u32[]{:S(2)}) collective-permute-start(s32[4,8]{1,0:T(4,128)} %refs_4_), channel_id=1, source_target_pairs={{0,64},{32,96},{64,0},{96,32},{1,65},{33,97},{65,1},{97,33},{2,66}... | collective-permute-start | bytes 392 | tf_op jit(solution)/shard_map/ppermute | solution.py:579
  3.9 0.6 collective-permute-start
  4.5 2.6 %collective-permute-start.2 = (s32[4,8]{1,0:T(4,128)}, s32[4,8]{1,0:T(4,128)}, u32[]{:S(2)}, u32[]{:S(2)}) collective-permute-start(s32[4,8]{1,0:T(4,128)} %refs_4_), channel_id=1, source_target_pairs={{0,96},{32,0},{64,32},{96,64},{1,97},{33,1},{65,33},{97,65},{2,98}... | collective-permute-start | bytes 392 | tf_op jit(solution)/shard_map/ppermute | solution.py:579
  7.2 1.9 %collective-permute-done.refs_1_.refs_5_ = s32[4,8]{1,0:T(4,128)} collective-permute-done((s32[4,8]{1,0:T(4,128)}, s32[4,8]{1,0:T(4,128)}, u32[]{:S(2)}, u32[]{:S(2)}) %collective-permute-start) | collective-permute-done | bytes 160 | tf_op jit(solution)/shard_map/ppermute | solution.py:579
  9.0 0.0 collective-permute-done.3.refs_2_
  9.0 2.3 %shard_map.95 = (bf16[4,560,128]{2,1,0:T(8,128)(2,1)}, f32[32,128]{1,0:T(8,128)}) custom-call(s32[1]{0:T(128)} %bitcast.place_ref, s32[4,8]{1,0:T(4,128)} %refs_4_, s32[4,8]{1,0:T(4,128)} %collective-permute-done.refs_1_.refs_5_, s32[4,8]{1,0:T(4,128)} %collective-permute-done.1.refs_2_.refs_6_, s32[4,8]{1,0:T(4,128)} %collective-permute-done.2.refs_3_.refs_7_, ...), custom_call_target="tpu_custom_call" | custom-call | tf_op jit(solution)/shard_map/pallas_call | solution.py:255
  11.4 4.4 %all-to-all-start = ((bf16[4,560,128]{2,1,0:T(8,128)(2,1)}), bf16[4,560,128]{2,1,0:T(8,128)(2,1)}, u32[]{:S(2)}, u32[]{:S(2)}) async-start(bf16[4,560,128]{2,1,0:T(8,128)(2,1)} %get-tuple-element.53), calls=%async_computation | async-start | bytes 1146880 | tf_op jit(solution)/shard_map/all_to_all | solution.py:616
  15.7 5.7 %shard_map.96.refs_0_ = s32[1048576]{0:T(1024)} custom-call(s32[1]{0:T(128)} %bitcast.6.half_ref.refs_4_, s32[8,64]{1,0:T(8,128)} %bitcast.66, s32[1,64]{1,0:T(1,128)} %bitcast.71, s32[8,64]{1,0:T(8,128)} %collective-permute-done.3.refs_2_, s32[1,64]{1,0:T(1,128)} %collective-permute-done.4.refs_3_), custom_call_target="tpu_custom_call" | custom-call | tf_op jit(solution)/shard_map/pallas_call | solution.py:196
  21.4 4.2 %all-to-all-done.refs_1_ = bf16[4,560,128]{2,1,0:T(8,128)(2,1)} async-done(((bf16[4,560,128]{2,1,0:T(8,128)(2,1)}), bf16[4,560,128]{2,1,0:T(8,128)(2,1)}, u32[]{:S(2)}, u32[]{:S(2)}) %all-to-all-start) | async-done | bytes 573472 | tf_op jit(solution)/shard_map/all_to_all | solution.py:616
  25.6 2.8 %shard_map.97.refs_0_ = s32[1048576]{0:T(1024)} custom-call(s32[1]{0:T(128)} %bitcast.6.half_ref.refs_4_, s32[8,64]{1,0:T(8,128)} %bitcast.67, s32[1,64]{1,0:T(1,128)} %bitcast.72, s32[8,64]{1,0:T(8,128)} %collective-permute-done.3.refs_2_, s32[1,64]{1,0:T(1,128)} %collective-permute-done.4.refs_3_), custom_call_target="tpu_custom_call" | custom-call | tf_op jit(solution)/shard_map/pallas_call | solution.py:196
  28.4 5.4 %shard_map.98 = (f32[16,32,128]{2,1,0:T(8,128)}, bf16[66,128,128]{2,1,0:T(8,128)(2,1)}) custom-call(s32[1048576]{0:T(1024)} %shard_map.96.refs_0_, bf16[4,560,128]{2,1,0:T(8,128)(2,1)} %all-to-all-done.refs_1_, bf16[4,560,128]{2,1,0:T(8,128)(2,1)} %collective-permute-done.5.refs_2_, bf16[64,8192]{1,0:T(8,128)(2,1)} %bitcast.62, s32[1]{0:T(128)} %bitcast.6.half_ref.refs_4_), custom_call_target="tpu_custom_call" | custom-call | tf_op jit(solution)/shard_map/pallas_call | solution.py:552
  33.9 10.2 %all-to-all-start.1 = ((f32[16,32,128]{2,1,0:T(8,128)}), f32[16,32,128]{2,1,0:T(8,128)S(1)}, u32[]{:S(2)}, u32[]{:S(2)}) async-start(f32[16,32,128]{2,1,0:T(8,128)} %get-tuple-element.80), calls=%async_computation.1 | async-start | bytes 524288 | tf_op jit(solution)/shard_map/all_to_all | solution.py:632
  44.1 0.0 copy-start.1
  44.1 0.7 copy-done.1
  44.9 0.7 copy-done.2
  45.5 2.8 %shard_map.99 = (bf16[2,33,128,128]{3,2,1,0:T(8,128)(2,1)}, f32[32,128]{1,0:T(8,128)S(1)}, bf16[128,128]{1,0:T(8,128)(2,1)S(1)}) custom-call(s32[1]{0:T(128)} %bitcast.6.half_ref.refs_4_, bf16[64,8192]{1,0:T(8,128)(2,1)} %bitcast.63, f32[64,128]{1,0:T(8,128)S(1)} %bitcast.61, s32[4,8]{1,0:T(4,128)S(1)} %copy-done.2, ...), custom_call_target="tpu_custom_call" | custom-call | tf_op jit(solution)/shard_map/pallas_call | solution.py:333
  48.3 4.6 %all-to-all-done.1.refs_4_ = f32[16,32,128]{2,1,0:T(8,128)S(1)} async-done(((f32[16,32,128]{2,1,0:T(8,128)}), f32[16,32,128]{2,1,0:T(8,128)S(1)}, u32[]{:S(2)}, u32[]{:S(2)}) %all-to-all-start.1) | async-done | bytes 262176 | tf_op jit(solution)/shard_map/all_to_all | solution.py:632
  52.9 3.8 %shard_map.100 = f32[1,64,128]{2,1,0:T(8,128)S(1)} custom-call(s32[1048576]{0:T(1024)} %shard_map.97.refs_0_, bf16[4,560,128]{2,1,0:T(8,128)(2,1)} %all-to-all-done.refs_1_, bf16[4,560,128]{2,1,0:T(8,128)(2,1)} %collective-permute-done.5.refs_2_, bf16[2,33,128,128]{3,2,1,0:T(8,128)(2,1)} %get-tuple-element.78.refs_3_.refs_2_, ...), custom_call_target="tpu_custom_call" | custom-call | tf_op jit(solution)/shard_map/pallas_call | solution.py:552
  56.7 0.1 collective-permute-start.6
  56.8 0.5 collective-permute-start.10
  57.3 0.7 collective-permute-done.6
  58.0 4.1 %collective-permute-start.9 = (f32[64,128]{1,0:T(8,128)S(1)}, f32[64,128]{1,0:T(8,128)S(1)}, u32[]{:S(2)}, u32[]{:S(2)}) collective-permute-start(f32[64,128]{1,0:T(8,128)S(1)} %multiply_add_fusion.1.refs_3_), channel_id=1, source_target_pairs={{0,96},{32,0},{64,32},{96,64},{1,97},{33,1},{65,33},{97,65},{2,98}... | collective-permute-start | bytes 98312 | tf_op jit(solution)/shard_map/ppermute | solution.py:579
  62.2 0.9 collective-permute-start.7
  63.1 0.6 collective-permute-done.9.refs_6_
  63.7 3.9 %collective-permute-done.8.refs_5_ = f32[64,128]{1,0:T(8,128)S(1)} collective-permute-done((f32[64,128]{1,0:T(8,128)S(1)}, f32[64,128]{1,0:T(8,128)S(1)}, u32[]{:S(2)}, u32[]{:S(2)}) %collective-permute-start.8) | collective-permute-done | bytes 32800 | tf_op jit(solution)/shard_map/ppermute | solution.py:579
  67.6 0.0 collective-permute-done.7.refs_4_
  67.6 3.8 %shard_map.101 = f32[16,32,128]{2,1,0:T(8,128)S(1)} custom-call(s32[1048576]{0:T(1024)} %shard_map.96.refs_0_, bf16[66,128,128]{2,1,0:T(8,128)(2,1)} %get-tuple-element.79.refs_1_, bf16[2,33,128,128]{3,2,1,0:T(8,128)(2,1)} %get-tuple-element.78.refs_3_.refs_2_, f32[64,128]{1,0:T(8,128)S(1)} %multiply_add_fusion.1.refs_3_, ...), custom_call_target="tpu_custom_call" | custom-call | tf_op jit(solution)/shard_map/pallas_call | solution.py:552
  71.5 13.3 %all_to_all.20.refs_4_ = f32[16,32,128]{2,1,0:T(8,128)S(1)} all-to-all(f32[16,32,128]{2,1,0:T(8,128)S(1)} %shard_map.101), channel_id=1, replica_groups={{0,2,4,6,8,10,12,14,16,18,20,22,24,26,28,30},{1,3,5,7,9,11,13,15,17,19,..., dimensions={0} | all-to-all | bytes 524288 | tf_op jit(solution)/shard_map/all_to_all | solution.py:632
  84.8 3.8 %shard_map.102 = f32[1,64,128]{2,1,0:T(8,128)S(1)} custom-call(s32[1048576]{0:T(1024)} %shard_map.97.refs_0_, bf16[4,560,128]{2,1,0:T(8,128)(2,1)} %all-to-all-done.refs_1_, bf16[4,560,128]{2,1,0:T(8,128)(2,1)} %collective-permute-done.5.refs_2_, bf16[2,33,128,128]{3,2,1,0:T(8,128)(2,1)} %get-tuple-element.78.refs_3_.refs_2_, ...), custom_call_target="tpu_custom_call" | custom-call | tf_op jit(solution)/shard_map/pallas_call | solution.py:552
  88.6 0.1 collective-permute-start.11
  88.7 1.2 collective-permute-done.11
  89.9 4.0 %collective-permute-start.14 = (f32[64,128]{1,0:T(8,128)S(1)}, f32[64,128]{1,0:T(8,128)S(1)}, u32[]{:S(2)}, u32[]{:S(2)}) collective-permute-start(f32[64,128]{1,0:T(8,128)S(1)} %multiply_add_fusion.refs_3_), channel_id=1, source_target_pairs={{0,96},{32,0},{64,32},{96,64},{1,97},{33,1},{65,33},{97,65},{2,98}... | collective-permute-start | bytes 98312 | tf_op jit(solution)/shard_map/ppermute | solution.py:579
  93.9 0.9 collective-permute-start.12
  94.8 0.6 collective-permute-done.14.refs_6_
  95.5 3.9 %collective-permute-done.13.refs_5_ = f32[64,128]{1,0:T(8,128)S(1)} collective-permute-done((f32[64,128]{1,0:T(8,128)S(1)}, f32[64,128]{1,0:T(8,128)S(1)}, u32[]{:S(2)}, u32[]{:S(2)}) %collective-permute-start.13) | collective-permute-done | bytes 32800 | tf_op jit(solution)/shard_map/ppermute | solution.py:579
  99.3 0.0 collective-permute-done.12.refs_4_
  99.3 3.8 %shard_map.103 = f32[16,32,128]{2,1,0:T(8,128)S(1)} custom-call(s32[1048576]{0:T(1024)} %shard_map.96.refs_0_, bf16[66,128,128]{2,1,0:T(8,128)(2,1)} %get-tuple-element.79.refs_1_, bf16[2,33,128,128]{3,2,1,0:T(8,128)(2,1)} %get-tuple-element.78.refs_3_.refs_2_, f32[64,128]{1,0:T(8,128)S(1)} %multiply_add_fusion.refs_3_, ...), custom_call_target="tpu_custom_call" | custom-call | tf_op jit(solution)/shard_map/pallas_call | solution.py:552
  103.2 13.3 %all_to_all.21.refs_4_ = f32[16,32,128]{2,1,0:T(8,128)S(1)} all-to-all(f32[16,32,128]{2,1,0:T(8,128)S(1)} %shard_map.103), channel_id=1, replica_groups={{0,2,4,6,8,10,12,14,16,18,20,22,24,26,28,30},{1,3,5,7,9,11,13,15,17,19,..., dimensions={0} | all-to-all | bytes 524288 | tf_op jit(solution)/shard_map/all_to_all | solution.py:632
  116.5 4.0 %shard_map.104 = (f32[1,64,128]{2,1,0:T(8,128)S(1)}, f32[32,128]{1,0:T(8,128)S(1)}) custom-call(s32[1048576]{0:T(1024)} %shard_map.97.refs_0_, bf16[4,560,128]{2,1,0:T(8,128)(2,1)} %all-to-all-done.refs_1_, bf16[4,560,128]{2,1,0:T(8,128)(2,1)} %collective-permute-done.5.refs_2_, bf16[2,33,128,128]{3,2,1,0:T(8,128)(2,1)} %get-tuple-element.78.refs_3_.refs_2_, ...), custom_call_target="tpu_custom_call" | custom-call | tf_op jit(solution)/shard_map/pallas_call | solution.py:552
  120.5 0.1 collective-permute-start.16
  120.6 0.5 collective-permute-start.15
  121.1 0.7 collective-permute-done.16
  121.9 4.0 %collective-permute-start.19 = (f32[8,128]{1,0:T(8,128)S(1)}, f32[8,128]{1,0:T(8,128)S(1)}, u32[]{:S(2)}, u32[]{:S(2)}) collective-permute-start(f32[8,128]{1,0:T(8,128)S(1)} %get-tuple-element.102), channel_id=1, source_target_pairs={{0,96},{32,0},{64,32},{96,64},{1,97},{33,1},{65,33},{97,65},{2,98}... | collective-permute-start | bytes 12296 | tf_op jit(solution)/shard_map/ppermute | solution.py:656
  125.9 0.9 collective-permute-start.17
  126.9 0.6 maximum_bitcast_fusion
  127.5 3.5 %collective-permute-done.18.refs_2_ = f32[8,128]{1,0:T(8,128)S(1)} collective-permute-done((f32[8,128]{1,0:T(8,128)S(1)}, f32[8,128]{1,0:T(8,128)S(1)}, u32[]{:S(2)}, u32[]{:S(2)}) %collective-permute-start.18) | collective-permute-done | bytes 4128 | tf_op jit(solution)/shard_map/ppermute | solution.py:656
  131.0 1.5 %shard_map.105 = f32[32,128]{1,0:T(8,128)} custom-call(s32[1]{0:T(128)} %bitcast.15.place_ref, f32[8,128]{1,0:T(8,128)S(1)} %get-tuple-element.105.refs_0_, f32[8,128]{1,0:T(8,128)S(1)} %collective-permute-done.17.refs_1_, f32[8,128]{1,0:T(8,128)S(1)} %collective-permute-done.18.refs_2_, f32[8,128]{1,0:T(8,128)S(1)} %collective-permute-done.19.refs_3_, ...), custom_call_target="tpu_custom_call" | custom-call | tf_op jit(solution)/shard_map/pallas_call | solution.py:280
  (29 shorter events, 0.2 us)
Async XLA Ops:
  0.6 8.4 %collective-permute-start.3 = (s32[8,64]{1,0:T(8,128)}, s32[8,64]{1,0:T(8,128)}, u32[]{:S(2)}, u32[]{:S(2)}) collective-permute-start(s32[8,64]{1,0:T(8,128)} %bitcast.65), channel_id=1, source_target_pairs={{0,1},{1,0},{2,3},{3,2},{4,5},{5,4},{6,7},{7,6},{8,9},{9,8},{10,11... | collective-permute-start | bytes 6152 | tf_op jit(solution)/shard_map/ppermute | solution.py:579
  0.7 6.4 %collective-permute-start.1 = (s32[4,8]{1,0:T(4,128)}, s32[4,8]{1,0:T(4,128)}, u32[]{:S(2)}, u32[]{:S(2)}) collective-permute-start(s32[4,8]{1,0:T(4,128)} %refs_4_), channel_id=1, source_target_pairs={{0,64},{32,96},{64,0},{96,32},{1,65},{33,97},{65,1},{97,33},{2,66}... | collective-permute-start | bytes 392 | tf_op jit(solution)/shard_map/ppermute | solution.py:579
  3.9 5.1 %collective-permute-start = (s32[4,8]{1,0:T(4,128)}, s32[4,8]{1,0:T(4,128)}, u32[]{:S(2)}, u32[]{:S(2)}) collective-permute-start(s32[4,8]{1,0:T(4,128)} %refs_4_), channel_id=1, source_target_pairs={{0,32},{32,64},{64,96},{96,0},{1,33},{33,65},{65,97},{97,1},{2,34}... | collective-permute-start | bytes 392 | tf_op jit(solution)/shard_map/ppermute | solution.py:579
  4.5 4.5 %collective-permute-start.2 = (s32[4,8]{1,0:T(4,128)}, s32[4,8]{1,0:T(4,128)}, u32[]{:S(2)}, u32[]{:S(2)}) collective-permute-start(s32[4,8]{1,0:T(4,128)} %refs_4_), channel_id=1, source_target_pairs={{0,96},{32,0},{64,32},{96,64},{1,97},{33,1},{65,33},{97,65},{2,98}... | collective-permute-start | bytes 392 | tf_op jit(solution)/shard_map/ppermute | solution.py:579
  7.2 1.9 %collective-permute-start.4 = (s32[1,64]{1,0:T(1,128)}, s32[1,64]{1,0:T(1,128)}, u32[]{:S(2)}, u32[]{:S(2)}) collective-permute-start(s32[1,64]{1,0:T(1,128)} %bitcast.70), channel_id=1, source_target_pairs={{0,1},{1,0},{2,3},{3,2},{4,5},{5,4},{6,7},{7,6},{8,9},{9,8},{10,11... | collective-permute-start | bytes 776 | tf_op jit(solution)/shard_map/ppermute | solution.py:579
  11.4 14.3 %all-to-all-start = ((bf16[4,560,128]{2,1,0:T(8,128)(2,1)}), bf16[4,560,128]{2,1,0:T(8,128)(2,1)}, u32[]{:S(2)}, u32[]{:S(2)}) async-start(bf16[4,560,128]{2,1,0:T(8,128)(2,1)} %get-tuple-element.53), calls=%async_computation | async-start | bytes 1146880 | tf_op jit(solution)/shard_map/all_to_all | solution.py:616
  25.6 2.8 %collective-permute-start.5 = (bf16[4,560,128]{2,1,0:T(8,128)(2,1)}, bf16[4,560,128]{2,1,0:T(8,128)(2,1)}, u32[]{:S(2)}, u32[]{:S(2)}) collective-permute-start(bf16[4,560,128]{2,1,0:T(8,128)(2,1)} %all-to-all-done.refs_1_), channel_id=1, source_target_pairs={{0,1},{1,0},{2,3},{3,2},{4,5},{5,4},{6,7},{7,6},{8,9},{9,8},{10,11... | collective-permute-start | bytes 1720328 | tf_op jit(solution)/shard_map/ppermute | solution.py:579
  33.9 19.0 %all-to-all-start.1 = ((f32[16,32,128]{2,1,0:T(8,128)}), f32[16,32,128]{2,1,0:T(8,128)S(1)}, u32[]{:S(2)}, u32[]{:S(2)}) async-start(f32[16,32,128]{2,1,0:T(8,128)} %get-tuple-element.80), calls=%async_computation.1 | async-start | bytes 524288 | tf_op jit(solution)/shard_map/all_to_all | solution.py:632
  44.1 0.8 copy-start.1
  44.8 0.7 copy-start.2
  56.7 1.3 collective-permute-start.6
  56.8 6.3 %collective-permute-start.10 = (bf16[128,128]{1,0:T(8,128)(2,1)S(1)}, bf16[128,128]{1,0:T(8,128)(2,1)S(1)}, u32[]{:S(2)}, u32[]{:S(2)}) collective-permute-start(bf16[128,128]{1,0:T(8,128)(2,1)S(1)} %get-tuple-element.81.refs_7_), channel_id=1, source_target_pairs={{0,1},{1,0},{2,3},{3,2},{4,5},{5,4},{6,7},{7,6},{8,9},{9,8},{10,11... | collective-permute-start | bytes 98312 | tf_op jit(solution)/shard_map/ppermute | solution.py:579
  58.0 5.7 %collective-permute-start.9 = (f32[64,128]{1,0:T(8,128)S(1)}, f32[64,128]{1,0:T(8,128)S(1)}, u32[]{:S(2)}, u32[]{:S(2)}) collective-permute-start(f32[64,128]{1,0:T(8,128)S(1)} %multiply_add_fusion.1.refs_3_), channel_id=1, source_target_pairs={{0,96},{32,0},{64,32},{96,64},{1,97},{33,1},{65,33},{97,65},{2,98}... | collective-permute-start | bytes 98312 | tf_op jit(solution)/shard_map/ppermute | solution.py:579
  62.1 5.5 %collective-permute-start.8 = (f32[64,128]{1,0:T(8,128)S(1)}, f32[64,128]{1,0:T(8,128)S(1)}, u32[]{:S(2)}, u32[]{:S(2)}) collective-permute-start(f32[64,128]{1,0:T(8,128)S(1)} %multiply_add_fusion.1.refs_3_), channel_id=1, source_target_pairs={{0,64},{32,96},{64,0},{96,32},{1,65},{33,97},{65,1},{97,33},{2,66}... | collective-permute-start | bytes 98312 | tf_op jit(solution)/shard_map/ppermute | solution.py:579
  62.2 5.5 %collective-permute-start.7 = (f32[64,128]{1,0:T(8,128)S(1)}, f32[64,128]{1,0:T(8,128)S(1)}, u32[]{:S(2)}, u32[]{:S(2)}) collective-permute-start(f32[64,128]{1,0:T(8,128)S(1)} %multiply_add_fusion.1.refs_3_), channel_id=1, source_target_pairs={{0,32},{32,64},{64,96},{96,0},{1,33},{33,65},{65,97},{97,1},{2,34}... | collective-permute-start | bytes 98312 | tf_op jit(solution)/shard_map/ppermute | solution.py:579
  88.6 1.3 collective-permute-start.11
  89.9 5.6 %collective-permute-start.14 = (f32[64,128]{1,0:T(8,128)S(1)}, f32[64,128]{1,0:T(8,128)S(1)}, u32[]{:S(2)}, u32[]{:S(2)}) collective-permute-start(f32[64,128]{1,0:T(8,128)S(1)} %multiply_add_fusion.refs_3_), channel_id=1, source_target_pairs={{0,96},{32,0},{64,32},{96,64},{1,97},{33,1},{65,33},{97,65},{2,98}... | collective-permute-start | bytes 98312 | tf_op jit(solution)/shard_map/ppermute | solution.py:579
  93.9 5.5 %collective-permute-start.13 = (f32[64,128]{1,0:T(8,128)S(1)}, f32[64,128]{1,0:T(8,128)S(1)}, u32[]{:S(2)}, u32[]{:S(2)}) collective-permute-start(f32[64,128]{1,0:T(8,128)S(1)} %multiply_add_fusion.refs_3_), channel_id=1, source_target_pairs={{0,64},{32,96},{64,0},{96,32},{1,65},{33,97},{65,1},{97,33},{2,66}... | collective-permute-start | bytes 98312 | tf_op jit(solution)/shard_map/ppermute | solution.py:579
  93.9 5.5 %collective-permute-start.12 = (f32[64,128]{1,0:T(8,128)S(1)}, f32[64,128]{1,0:T(8,128)S(1)}, u32[]{:S(2)}, u32[]{:S(2)}) collective-permute-start(f32[64,128]{1,0:T(8,128)S(1)} %multiply_add_fusion.refs_3_), channel_id=1, source_target_pairs={{0,32},{32,64},{64,96},{96,0},{1,33},{33,65},{65,97},{97,1},{2,34}... | collective-permute-start | bytes 98312 | tf_op jit(solution)/shard_map/ppermute | solution.py:579
  116.5 14.5 %copy-start = (f32[4096]{0:T(1024)S(1)}, f32[4096]{0:T(1024)}, u32[]{:S(2)}) copy-start(f32[4096]{0:T(1024)} %param.11) | copy-start | bytes 49156
  116.5 14.5 %copy-start.3 = (s32[4,8]{1,0:T(4,128)S(1)}, s32[4,8]{1,0:T(4,128)}, u32[]{:S(2)}) copy-start(s32[4,8]{1,0:T(4,128)} %refs_4_) | copy-start | bytes 388
  116.5 14.5 %copy-start.4 = (f32[32,128]{1,0:T(8,128)S(1)}, f32[32,128]{1,0:T(8,128)}, u32[]{:S(2)}) copy-start(f32[32,128]{1,0:T(8,128)} %get-tuple-element.95.refs_9_) | copy-start | bytes 49156
  120.5 1.3 collective-permute-start.16
  120.6 6.2 %collective-permute-start.15 = (f32[32,128]{1,0:T(8,128)S(1)}, f32[32,128]{1,0:T(8,128)S(1)}, u32[]{:S(2)}, u32[]{:S(2)}) collective-permute-start(f32[32,128]{1,0:T(8,128)S(1)} %multiply_add_fusion.2), channel_id=1, source_target_pairs={{0,1},{1,0},{2,3},{3,2},{4,5},{5,4},{6,7},{7,6},{8,9},{9,8},{10,11... | collective-permute-start | bytes 49160 | tf_op jit(solution)/shard_map/ppermute | solution.py:579
  121.9 5.6 %collective-permute-start.19 = (f32[8,128]{1,0:T(8,128)S(1)}, f32[8,128]{1,0:T(8,128)S(1)}, u32[]{:S(2)}, u32[]{:S(2)}) collective-permute-start(f32[8,128]{1,0:T(8,128)S(1)} %get-tuple-element.102), channel_id=1, source_target_pairs={{0,96},{32,0},{64,32},{96,64},{1,97},{33,1},{65,33},{97,65},{2,98}... | collective-permute-start | bytes 12296 | tf_op jit(solution)/shard_map/ppermute | solution.py:656
  125.9 5.1 %collective-permute-start.18 = (f32[8,128]{1,0:T(8,128)S(1)}, f32[8,128]{1,0:T(8,128)S(1)}, u32[]{:S(2)}, u32[]{:S(2)}) collective-permute-start(f32[8,128]{1,0:T(8,128)S(1)} %get-tuple-element.103), channel_id=1, source_target_pairs={{0,64},{32,96},{64,0},{96,32},{1,65},{33,97},{65,1},{97,33},{2,66}... | collective-permute-start | bytes 12296 | tf_op jit(solution)/shard_map/ppermute | solution.py:656
  125.9 5.1 %collective-permute-start.17 = (f32[8,128]{1,0:T(8,128)S(1)}, f32[8,128]{1,0:T(8,128)S(1)}, u32[]{:S(2)}, u32[]{:S(2)}) collective-permute-start(f32[8,128]{1,0:T(8,128)S(1)} %get-tuple-element.104), channel_id=1, source_target_pairs={{0,32},{32,64},{64,96},{96,0},{1,33},{33,65},{65,97},{97,1},{2,34}... | collective-permute-start | bytes 12296 | tf_op jit(solution)/shard_map/ppermute | solution.py:656
where the time goes:
time: 134 us; the launch traced here: 132 us
  Pallas kernels  39.7 us (30%)
  starting transfers between devices  37.2 us (28%)
  blocking collectives  26.6 us (20%)
  waiting for transfers between devices  25.8 us (19%)
  local copies, waits for them, and re-layouts  1.47 us (1%)
    all_to_all x2, blocking collectives, shards(): lax.all_to_all(rows, 'grp', split_axis=0, concat_axis=0, tiled=True, axis...  26.6 us
    pallas_call x6, Pallas kernels, log_sums(): pl.pallas_call(functools.partial(pass_kernel, kind), out_shape=outs, in_s...  24.7 us
    ppermute x17, starting transfers between devices, ring(): out.append(lax.ppermute(values, axis, pairs))  17.8 us
    ppermute x17, waiting for transfers between devices, ring(): out.append(lax.ppermute(values, axis, pairs))  13.5 us
    all_to_all x1, starting transfers between devices, shards(): lax.all_to_all(rows, 'grp', split_axis=0, concat_axis=0, tiled=True, axis...  10.2 us
    pallas_call x2, Pallas kernels, make_list(): pl.pallas_call(kernel, out_shape=shape((LONG,), jnp.int32), in_specs=[SME...  8.49 us
    ppermute x3, starting transfers between devices, shards(): back.append(wanted if d == 0 else lax.ppermute(wanted, 'src', pairs))  4.95 us
    all_to_all x1, waiting for transfers between devices, shards(): lax.all_to_all(rows, 'grp', split_axis=0, concat_axis=0, tiled=True, axis...  4.59 us
  transfers between devices with their start and end apart: 22, of which 11 were waited for; matrix products, arithmetic and copies ran while one was open for 1% of the time, Pallas kernels for 8%

commit v1 on v0

--- a/solution.py
+++ b/solution.py
@@ -459,7 +459,7 @@
             columns[group * GROUP + k] = jnp.where(lane == k, turned, 0.0).astype(jnp.bfloat16)
             return carry
 
-        lax.fori_loop(0, GROUP, fill, 0, unroll=4)
+        lax.fori_loop(0, GROUP, fill, 0, unroll=8)
     for copy in copies[len(early) : len(early) + len(late)]:
         copy.wait()
     rights_at = HEAD + (list_ref.shape[0] - HEAD) // 3
@@ -523,7 +523,7 @@
         out_ref[0, pl.ds(pl.multiple_of(octet * 8, 8), 8), :] = jnp.concatenate(rows, axis=0)
         return carry
 
-    lax.fori_loop(0, rights // 8, finish, 0)
+    lax.fori_loop(0, rights // 8, finish, 0, unroll=4)
     for k in range(1, out_ref.shape[0]):
         out_ref[k] = out_ref[0]
     if kind == FIRST:
@@ -613,10 +613,10 @@
         target_logmass.reshape(owned, BLOCK),
     )
     row_pairs = make_list(rows_kernel, half, tiles)
+    col_pairs = make_list(columns_kernel, half, tiles)
     fetched = lax.all_to_all(packed, "src", split_axis=0, concat_axis=0, tiled=True)
-    fetched, row_pairs, ids, tiles = lax.optimization_barrier((fetched, row_pairs, ids, tiles))
-    col_pairs = make_list(columns_kernel, half, tiles)
-    *both, col_pairs = lax.optimization_barrier((fetched, swap(fetched), col_pairs))
+    fetched, row_pairs, col_pairs, ids = lax.optimization_barrier((fetched, row_pairs, col_pairs, ids))
+    both = lax.optimization_barrier([fetched, swap(fetched)])
 
     groups = lax.axis_size("grp")
     same_core = [list(range(core, groups, 2)) for core in range(2)]

time: 134 us -> 130 us (0.970)
  starting transfers between devices: 37.2 us -> 30.6 us
  blocking collectives: 26.6 us -> 31.5 us
  waiting for transfers between devices: 25.8 us -> 24.2 us
    all_to_all x2, blocking collectives: 26.6 us -> 31.5 us  [shards(): lax.all_to_all(rows, 'grp', split_axis=0, concat_axis=0, tiled=True, axis...]
    ppermute x17, starting transfers between devices: 17.8 us -> 14 us  [ring(): out.append(lax.ppermute(values, axis, pairs))]
    ppermute x3, starting transfers between devices: 4.95 us -> 2.09 us  [shards(): back.append(wanted if d == 0 else lax.ppermute(wanted, 'src', pairs))]
    all_to_all x1, waiting for transfers between devices: 4.2 us -> 1.53 us  [shards(): lax.all_to_all(packed, 'src', split_axis=0, concat_axis=0, tiled=True)]
  transfers between devices with their start and end apart: 22 -> 22, of which waited for: 11 -> 16; matrix products, arithmetic and copies ran while one was open for 1% -> 1% of each run, Pallas kernels for 8% -> 9%
where the time goes in v1:
time: 130 us; the launch traced here: 129 us
  Pallas kernels  39.3 us (30%)
  blocking collectives  31.5 us (24%)
  starting transfers between devices  30.6 us (24%)
  waiting for transfers between devices  24.2 us (19%)
  local copies, waits for them, and re-layouts  1.47 us (1%)
    all_to_all x2, blocking collectives, shards(): lax.all_to_all(rows, 'grp', split_axis=0, concat_axis=0, tiled=True, axis...  31.5 us
    pallas_call x6, Pallas kernels, log_sums(): pl.pallas_call(functools.partial(pass_kernel, kind), out_shape=outs, in_s...  24.2 us
    ppermute x17, waiting for transfers between devices, ring(): out.append(lax.ppermute(values, axis, pairs))  14.5 us
    ppermute x17, starting transfers between devices, ring(): out.append(lax.ppermute(values, axis, pairs))  14 us
    all_to_all x1, starting transfers between devices, shards(): lax.all_to_all(rows, 'grp', split_axis=0, concat_axis=0, tiled=True, axis...  10.1 us
    pallas_call x2, Pallas kernels, make_list(): pl.pallas_call(kernel, out_shape=shape((LONG,), jnp.int32), in_specs=[SME...  8.49 us
    all_to_all x1, waiting for transfers between devices, shards(): lax.all_to_all(rows, 'grp', split_axis=0, concat_axis=0, tiled=True, axis...  4.48 us
    all_to_all x1, starting transfers between devices, shards(): lax.all_to_all(packed, 'src', split_axis=0, concat_axis=0, tiled=True)  4.36 us
  transfers between devices with their start and end apart: 22, of which 16 were waited for; matrix products, arithmetic and copies ran while one was open for 1% of the time, Pallas kernels for 9%

profile of v1, /device:TPU:0, one launch (start us, length us, event | category | flops | bytes accessed | tf_op | source)
XLA Modules:
  0.0 128.7 jit_solution(10286963112954819730)
XLA Ops:
  0.6 0.1 collective-permute-start.3
  0.7 3.2 %collective-permute-start.1 = (s32[4,8]{1,0:T(4,128)}, s32[4,8]{1,0:T(4,128)}, u32[]{:S(2)}, u32[]{:S(2)}) collective-permute-start(s32[4,8]{1,0:T(4,128)} %refs_4_), channel_id=1, source_target_pairs={{0,64},{32,96},{64,0},{96,32},{1,65},{33,97},{65,1},{97,33},{2,66}... | collective-permute-start | bytes 392 | tf_op jit(solution)/shard_map/ppermute | solution.py:579
  3.9 0.6 collective-permute-start
  4.5 2.6 %collective-permute-start.2 = (s32[4,8]{1,0:T(4,128)}, s32[4,8]{1,0:T(4,128)}, u32[]{:S(2)}, u32[]{:S(2)}) collective-permute-start(s32[4,8]{1,0:T(4,128)} %refs_4_), channel_id=1, source_target_pairs={{0,96},{32,0},{64,32},{96,64},{1,97},{33,1},{65,33},{97,65},{2,98}... | collective-permute-start | bytes 392 | tf_op jit(solution)/shard_map/ppermute | solution.py:579
  7.2 1.9 %collective-permute-done.refs_1_.refs_5_ = s32[4,8]{1,0:T(4,128)} collective-permute-done((s32[4,8]{1,0:T(4,128)}, s32[4,8]{1,0:T(4,128)}, u32[]{:S(2)}, u32[]{:S(2)}) %collective-permute-start) | collective-permute-done | bytes 160 | tf_op jit(solution)/shard_map/ppermute | solution.py:579
  9.0 2.4 %shard_map.95 = (bf16[4,560,128]{2,1,0:T(8,128)(2,1)}, f32[32,128]{1,0:T(8,128)}) custom-call(s32[1]{0:T(128)} %bitcast.place_ref, s32[4,8]{1,0:T(4,128)} %refs_4_, s32[4,8]{1,0:T(4,128)} %collective-permute-done.refs_1_.refs_5_, s32[4,8]{1,0:T(4,128)} %collective-permute-done.1.refs_2_.refs_6_, s32[4,8]{1,0:T(4,128)} %collective-permute-done.2.refs_3_.refs_7_, ...), custom_call_target="tpu_custom_call" | custom-call | tf_op jit(solution)/shard_map/pallas_call | solution.py:255
  11.4 4.4 %all-to-all-start = ((bf16[4,560,128]{2,1,0:T(8,128)(2,1)}), bf16[4,560,128]{2,1,0:T(8,128)(2,1)}, u32[]{:S(2)}, u32[]{:S(2)}) async-start(bf16[4,560,128]{2,1,0:T(8,128)(2,1)} %get-tuple-element.49), calls=%async_computation | async-start | bytes 1146880 | tf_op jit(solution)/shard_map/all_to_all | solution.py:617
  15.8 2.8 %shard_map.97.refs_0_ = s32[1048576]{0:T(1024)} custom-call(s32[1]{0:T(128)} %bitcast.6.half_ref.refs_4_, s32[8,64]{1,0:T(8,128)} %bitcast.66, s32[1,64]{1,0:T(1,128)} %bitcast.71, s32[8,64]{1,0:T(8,128)} %collective-permute-done.3.refs_2_, s32[1,64]{1,0:T(1,128)} %collective-permute-done.4.refs_3_), custom_call_target="tpu_custom_call" | custom-call | tf_op jit(solution)/shard_map/pallas_call | solution.py:196
  18.6 5.7 %shard_map.96.refs_0_ = s32[1048576]{0:T(1024)} custom-call(s32[1]{0:T(128)} %bitcast.6.half_ref.refs_4_, s32[8,64]{1,0:T(8,128)} %bitcast.67, s32[1,64]{1,0:T(1,128)} %bitcast.72, s32[8,64]{1,0:T(8,128)} %collective-permute-done.3.refs_2_, s32[1,64]{1,0:T(1,128)} %collective-permute-done.4.refs_3_), custom_call_target="tpu_custom_call" | custom-call | tf_op jit(solution)/shard_map/pallas_call | solution.py:196
  24.3 1.5 %all-to-all-done.refs_1_ = bf16[4,560,128]{2,1,0:T(8,128)(2,1)} async-done(((bf16[4,560,128]{2,1,0:T(8,128)(2,1)}), bf16[4,560,128]{2,1,0:T(8,128)(2,1)}, u32[]{:S(2)}, u32[]{:S(2)}) %all-to-all-start) | async-done | bytes 573472 | tf_op jit(solution)/shard_map/all_to_all | solution.py:617
  25.8 2.3 %collective-permute-done.5.refs_2_ = bf16[4,560,128]{2,1,0:T(8,128)(2,1)} collective-permute-done((bf16[4,560,128]{2,1,0:T(8,128)(2,1)}, bf16[4,560,128]{2,1,0:T(8,128)(2,1)}, u32[]{:S(2)}, u32[]{:S(2)}) %collective-permute-start.5) | collective-permute-done | bytes 573472 | tf_op jit(solution)/shard_map/ppermute | solution.py:579
  28.1 5.4 %shard_map.98 = (f32[16,32,128]{2,1,0:T(8,128)}, bf16[66,128,128]{2,1,0:T(8,128)(2,1)}) custom-call(s32[1048576]{0:T(1024)} %shard_map.96.refs_0_, bf16[4,560,128]{2,1,0:T(8,128)(2,1)} %all-to-all-done.refs_1_, bf16[4,560,128]{2,1,0:T(8,128)(2,1)} %collective-permute-done.5.refs_2_, bf16[64,8192]{1,0:T(8,128)(2,1)} %bitcast.62, s32[1]{0:T(128)} %bitcast.6.half_ref.refs_4_), custom_call_target="tpu_custom_call" | custom-call | tf_op jit(solution)/shard_map/pallas_call | solution.py:552
  33.5 10.1 %all-to-all-start.1 = ((f32[16,32,128]{2,1,0:T(8,128)}), f32[16,32,128]{2,1,0:T(8,128)S(1)}, u32[]{:S(2)}, u32[]{:S(2)}) async-start(f32[16,32,128]{2,1,0:T(8,128)} %get-tuple-element.72), calls=%async_computation.1 | async-start | bytes 524288 | tf_op jit(solution)/shard_map/all_to_all | solution.py:632
  43.7 0.7 copy-done.1
  44.4 0.7 copy-done.2
  45.1 2.8 %shard_map.99 = (bf16[2,33,128,128]{3,2,1,0:T(8,128)(2,1)}, f32[32,128]{1,0:T(8,128)S(1)}, bf16[128,128]{1,0:T(8,128)(2,1)S(1)}) custom-call(s32[1]{0:T(128)} %bitcast.6.half_ref.refs_4_, bf16[64,8192]{1,0:T(8,128)(2,1)} %bitcast.63, f32[64,128]{1,0:T(8,128)S(1)} %bitcast.61, s32[4,8]{1,0:T(4,128)S(1)} %copy-done.2, ...), custom_call_target="tpu_custom_call" | custom-call | tf_op jit(solution)/shard_map/pallas_call | solution.py:333
  47.9 4.5 %all-to-all-done.1.refs_4_ = f32[16,32,128]{2,1,0:T(8,128)S(1)} async-done(((f32[16,32,128]{2,1,0:T(8,128)}), f32[16,32,128]{2,1,0:T(8,128)S(1)}, u32[]{:S(2)}, u32[]{:S(2)}) %all-to-all-start.1) | async-done | bytes 262176 | tf_op jit(solution)/shard_map/all_to_all | solution.py:632
  52.3 3.7 %shard_map.100 = f32[1,64,128]{2,1,0:T(8,128)S(1)} custom-call(s32[1048576]{0:T(1024)} %shard_map.97.refs_0_, bf16[4,560,128]{2,1,0:T(8,128)(2,1)} %all-to-all-done.refs_1_, bf16[4,560,128]{2,1,0:T(8,128)(2,1)} %collective-permute-done.5.refs_2_, bf16[2,33,128,128]{3,2,1,0:T(8,128)(2,1)} %get-tuple-element.70.refs_3_.refs_2_, ...), custom_call_target="tpu_custom_call" | custom-call | tf_op jit(solution)/shard_map/pallas_call | solution.py:552
  56.1 0.5 collective-permute-start.10
  56.6 0.7 collective-permute-done.6
  57.4 0.1 collective-permute-start.9
  57.5 2.2 %collective-permute-start.8 = (f32[64,128]{1,0:T(8,128)S(1)}, f32[64,128]{1,0:T(8,128)S(1)}, u32[]{:S(2)}, u32[]{:S(2)}) collective-permute-start(f32[64,128]{1,0:T(8,128)S(1)} %multiply_add_fusion.1.refs_3_), channel_id=1, source_target_pairs={{0,64},{32,96},{64,0},{96,32},{1,65},{33,97},{65,1},{97,33},{2,66}... | collective-permute-start | bytes 98312 | tf_op jit(solution)/shard_map/ppermute | solution.py:579
  59.7 1.3 %collective-permute-start.7 = (f32[64,128]{1,0:T(8,128)S(1)}, f32[64,128]{1,0:T(8,128)S(1)}, u32[]{:S(2)}, u32[]{:S(2)}) collective-permute-start(f32[64,128]{1,0:T(8,128)S(1)} %multiply_add_fusion.1.refs_3_), channel_id=1, source_target_pairs={{0,32},{32,64},{64,96},{96,0},{1,33},{33,65},{65,97},{97,1},{2,34}... | collective-permute-start | bytes 98312 | tf_op jit(solution)/shard_map/ppermute | solution.py:579
  61.0 0.4 collective-permute-done.9.refs_6_
  61.3 1.6 %collective-permute-done.8.refs_5_ = f32[64,128]{1,0:T(8,128)S(1)} collective-permute-done((f32[64,128]{1,0:T(8,128)S(1)}, f32[64,128]{1,0:T(8,128)S(1)}, u32[]{:S(2)}, u32[]{:S(2)}) %collective-permute-start.8) | collective-permute-done | bytes 32800 | tf_op jit(solution)/shard_map/ppermute | solution.py:579
  62.9 1.8 %collective-permute-done.7.refs_4_ = f32[64,128]{1,0:T(8,128)S(1)} collective-permute-done((f32[64,128]{1,0:T(8,128)S(1)}, f32[64,128]{1,0:T(8,128)S(1)}, u32[]{:S(2)}, u32[]{:S(2)}) %collective-permute-start.7) | collective-permute-done | bytes 32800 | tf_op jit(solution)/shard_map/ppermute | solution.py:579
  64.8 3.8 %shard_map.101 = f32[16,32,128]{2,1,0:T(8,128)S(1)} custom-call(s32[1048576]{0:T(1024)} %shard_map.96.refs_0_, bf16[66,128,128]{2,1,0:T(8,128)(2,1)} %get-tuple-element.71.refs_1_, bf16[2,33,128,128]{3,2,1,0:T(8,128)(2,1)} %get-tuple-element.70.refs_3_.refs_2_, f32[64,128]{1,0:T(8,128)S(1)} %multiply_add_fusion.1.refs_3_, ...), custom_call_target="tpu_custom_call" | custom-call | tf_op jit(solution)/shard_map/pallas_call | solution.py:552
  68.6 15.5 %all_to_all.20.refs_4_ = f32[16,32,128]{2,1,0:T(8,128)S(1)} all-to-all(f32[16,32,128]{2,1,0:T(8,128)S(1)} %shard_map.101), channel_id=1, replica_groups={{0,2,4,6,8,10,12,14,16,18,20,22,24,26,28,30},{1,3,5,7,9,11,13,15,17,19,..., dimensions={0} | all-to-all | bytes 524288 | tf_op jit(solution)/shard_map/all_to_all | solution.py:632
  84.0 3.7 %shard_map.102 = f32[1,64,128]{2,1,0:T(8,128)S(1)} custom-call(s32[1048576]{0:T(1024)} %shard_map.97.refs_0_, bf16[4,560,128]{2,1,0:T(8,128)(2,1)} %all-to-all-done.refs_1_, bf16[4,560,128]{2,1,0:T(8,128)(2,1)} %collective-permute-done.5.refs_2_, bf16[2,33,128,128]{3,2,1,0:T(8,128)(2,1)} %get-tuple-element.70.refs_3_.refs_2_, ...), custom_call_target="tpu_custom_call" | custom-call | tf_op jit(solution)/shard_map/pallas_call | solution.py:552
  87.8 1.2 collective-permute-done.11
  89.0 0.2 collective-permute-start.14
  89.3 1.1 collective-permute-start.13
  90.4 1.3 %collective-permute-start.12 = (f32[64,128]{1,0:T(8,128)S(1)}, f32[64,128]{1,0:T(8,128)S(1)}, u32[]{:S(2)}, u32[]{:S(2)}) collective-permute-start(f32[64,128]{1,0:T(8,128)S(1)} %multiply_add_fusion.refs_3_), channel_id=1, source_target_pairs={{0,32},{32,64},{64,96},{96,0},{1,33},{33,65},{65,97},{97,1},{2,34}... | collective-permute-start | bytes 98312 | tf_op jit(solution)/shard_map/ppermute | solution.py:579
  91.7 1.3 %collective-permute-done.14.refs_6_ = f32[64,128]{1,0:T(8,128)S(1)} collective-permute-done((f32[64,128]{1,0:T(8,128)S(1)}, f32[64,128]{1,0:T(8,128)S(1)}, u32[]{:S(2)}, u32[]{:S(2)}) %collective-permute-start.14) | collective-permute-done | bytes 32800 | tf_op jit(solution)/shard_map/ppermute | solution.py:579
  93.0 1.8 %collective-permute-done.13.refs_5_ = f32[64,128]{1,0:T(8,128)S(1)} collective-permute-done((f32[64,128]{1,0:T(8,128)S(1)}, f32[64,128]{1,0:T(8,128)S(1)}, u32[]{:S(2)}, u32[]{:S(2)}) %collective-permute-start.13) | collective-permute-done | bytes 32800 | tf_op jit(solution)/shard_map/ppermute | solution.py:579
  94.8 0.9 collective-permute-done.12.refs_4_
  95.7 3.8 %shard_map.103 = f32[16,32,128]{2,1,0:T(8,128)S(1)} custom-call(s32[1048576]{0:T(1024)} %shard_map.96.refs_0_, bf16[66,128,128]{2,1,0:T(8,128)(2,1)} %get-tuple-element.71.refs_1_, bf16[2,33,128,128]{3,2,1,0:T(8,128)(2,1)} %get-tuple-element.70.refs_3_.refs_2_, f32[64,128]{1,0:T(8,128)S(1)} %multiply_add_fusion.refs_3_, ...), custom_call_target="tpu_custom_call" | custom-call | tf_op jit(solution)/shard_map/pallas_call | solution.py:552
  99.5 16.1 %all_to_all.21.refs_4_ = f32[16,32,128]{2,1,0:T(8,128)S(1)} all-to-all(f32[16,32,128]{2,1,0:T(8,128)S(1)} %shard_map.103), channel_id=1, replica_groups={{0,2,4,6,8,10,12,14,16,18,20,22,24,26,28,30},{1,3,5,7,9,11,13,15,17,19,..., dimensions={0} | all-to-all | bytes 524288 | tf_op jit(solution)/shard_map/all_to_all | solution.py:632
  115.6 4.0 %shard_map.104 = (f32[1,64,128]{2,1,0:T(8,128)S(1)}, f32[32,128]{1,0:T(8,128)S(1)}) custom-call(s32[1048576]{0:T(1024)} %shard_map.97.refs_0_, bf16[4,560,128]{2,1,0:T(8,128)(2,1)} %all-to-all-done.refs_1_, bf16[4,560,128]{2,1,0:T(8,128)(2,1)} %collective-permute-done.5.refs_2_, bf16[2,33,128,128]{3,2,1,0:T(8,128)(2,1)} %get-tuple-element.70.refs_3_.refs_2_, ...), custom_call_target="tpu_custom_call" | custom-call | tf_op jit(solution)/shard_map/pallas_call | solution.py:552
  119.7 0.5 collective-permute-start.15
  120.1 0.7 collective-permute-done.16
  121.0 0.8 collective-permute-start.18
  121.8 1.2 collective-permute-start.17
  123.0 0.6 maximum_bitcast_fusion
  123.6 0.9 collective-permute-done.19.refs_3_
  124.6 1.6 %collective-permute-done.18.refs_2_ = f32[8,128]{1,0:T(8,128)S(1)} collective-permute-done((f32[8,128]{1,0:T(8,128)S(1)}, f32[8,128]{1,0:T(8,128)S(1)}, u32[]{:S(2)}, u32[]{:S(2)}) %collective-permute-start.18) | collective-permute-done | bytes 4128 | tf_op jit(solution)/shard_map/ppermute | solution.py:656
  126.2 1.0 collective-permute-done.17.refs_1_
  127.3 1.5 %shard_map.105 = f32[32,128]{1,0:T(8,128)} custom-call(s32[1]{0:T(128)} %bitcast.15.place_ref, f32[8,128]{1,0:T(8,128)S(1)} %get-tuple-element.97.refs_0_, f32[8,128]{1,0:T(8,128)S(1)} %collective-permute-done.17.refs_1_, f32[8,128]{1,0:T(8,128)S(1)} %collective-permute-done.18.refs_2_, f32[8,128]{1,0:T(8,128)S(1)} %collective-permute-done.19.refs_3_, ...), custom_call_target="tpu_custom_call" | custom-call | tf_op jit(solution)/shard_map/pallas_call | solution.py:280
  (29 shorter events, 0.5 us)
Async XLA Ops:
  0.6 8.4 %collective-permute-start.3 = (s32[8,64]{1,0:T(8,128)}, s32[8,64]{1,0:T(8,128)}, u32[]{:S(2)}, u32[]{:S(2)}) collective-permute-start(s32[8,64]{1,0:T(8,128)} %bitcast.65), channel_id=1, source_target_pairs={{0,1},{1,0},{2,3},{3,2},{4,5},{5,4},{6,7},{7,6},{8,9},{9,8},{10,11... | collective-permute-start | bytes 6152 | tf_op jit(solution)/shard_map/ppermute | solution.py:579
  0.7 6.4 %collective-permute-start.1 = (s32[4,8]{1,0:T(4,128)}, s32[4,8]{1,0:T(4,128)}, u32[]{:S(2)}, u32[]{:S(2)}) collective-permute-start(s32[4,8]{1,0:T(4,128)} %refs_4_), channel_id=1, source_target_pairs={{0,64},{32,96},{64,0},{96,32},{1,65},{33,97},{65,1},{97,33},{2,66}... | collective-permute-start | bytes 392 | tf_op jit(solution)/shard_map/ppermute | solution.py:579
  3.9 5.1 %collective-permute-start = (s32[4,8]{1,0:T(4,128)}, s32[4,8]{1,0:T(4,128)}, u32[]{:S(2)}, u32[]{:S(2)}) collective-permute-start(s32[4,8]{1,0:T(4,128)} %refs_4_), channel_id=1, source_target_pairs={{0,32},{32,64},{64,96},{96,0},{1,33},{33,65},{65,97},{97,1},{2,34}... | collective-permute-start | bytes 392 | tf_op jit(solution)/shard_map/ppermute | solution.py:579
  4.5 4.5 %collective-permute-start.2 = (s32[4,8]{1,0:T(4,128)}, s32[4,8]{1,0:T(4,128)}, u32[]{:S(2)}, u32[]{:S(2)}) collective-permute-start(s32[4,8]{1,0:T(4,128)} %refs_4_), channel_id=1, source_target_pairs={{0,96},{32,0},{64,32},{96,64},{1,97},{33,1},{65,33},{97,65},{2,98}... | collective-permute-start | bytes 392 | tf_op jit(solution)/shard_map/ppermute | solution.py:579
  7.2 1.9 %collective-permute-start.4 = (s32[1,64]{1,0:T(1,128)}, s32[1,64]{1,0:T(1,128)}, u32[]{:S(2)}, u32[]{:S(2)}) collective-permute-start(s32[1,64]{1,0:T(1,128)} %bitcast.70), channel_id=1, source_target_pairs={{0,1},{1,0},{2,3},{3,2},{4,5},{5,4},{6,7},{7,6},{8,9},{9,8},{10,11... | collective-permute-start | bytes 776 | tf_op jit(solution)/shard_map/ppermute | solution.py:579
  11.4 14.4 %all-to-all-start = ((bf16[4,560,128]{2,1,0:T(8,128)(2,1)}), bf16[4,560,128]{2,1,0:T(8,128)(2,1)}, u32[]{:S(2)}, u32[]{:S(2)}) async-start(bf16[4,560,128]{2,1,0:T(8,128)(2,1)} %get-tuple-element.49), calls=%async_computation | async-start | bytes 1146880 | tf_op jit(solution)/shard_map/all_to_all | solution.py:617
  25.8 2.3 %collective-permute-start.5 = (bf16[4,560,128]{2,1,0:T(8,128)(2,1)}, bf16[4,560,128]{2,1,0:T(8,128)(2,1)}, u32[]{:S(2)}, u32[]{:S(2)}) collective-permute-start(bf16[4,560,128]{2,1,0:T(8,128)(2,1)} %all-to-all-done.refs_1_), channel_id=1, source_target_pairs={{0,1},{1,0},{2,3},{3,2},{4,5},{5,4},{6,7},{7,6},{8,9},{9,8},{10,11... | collective-permute-start | bytes 1720328 | tf_op jit(solution)/shard_map/ppermute | solution.py:579
  33.5 18.8 %all-to-all-start.1 = ((f32[16,32,128]{2,1,0:T(8,128)}), f32[16,32,128]{2,1,0:T(8,128)S(1)}, u32[]{:S(2)}, u32[]{:S(2)}) async-start(f32[16,32,128]{2,1,0:T(8,128)} %get-tuple-element.72), calls=%async_computation.1 | async-start | bytes 524288 | tf_op jit(solution)/shard_map/all_to_all | solution.py:632
  43.6 0.8 copy-start.1
  44.4 0.7 copy-start.2
  56.0 1.3 %collective-permute-start.6 = (f32[64,128]{1,0:T(8,128)S(1)}, f32[64,128]{1,0:T(8,128)S(1)}, u32[]{:S(2)}, u32[]{:S(2)}) collective-permute-start(f32[64,128]{1,0:T(8,128)S(1)} %bitcast.57), channel_id=1, source_target_pairs={{0,1},{1,0},{2,3},{3,2},{4,5},{5,4},{6,7},{7,6},{8,9},{9,8},{10,11... | collective-permute-start | bytes 98312 | tf_op jit(solution)/shard_map/ppermute | solution.py:579
  56.1 4.9 %collective-permute-start.10 = (bf16[128,128]{1,0:T(8,128)(2,1)S(1)}, bf16[128,128]{1,0:T(8,128)(2,1)S(1)}, u32[]{:S(2)}, u32[]{:S(2)}) collective-permute-start(bf16[128,128]{1,0:T(8,128)(2,1)S(1)} %get-tuple-element.73.refs_7_), channel_id=1, source_target_pairs={{0,1},{1,0},{2,3},{3,2},{4,5},{5,4},{6,7},{7,6},{8,9},{9,8},{10,11... | collective-permute-start | bytes 98312 | tf_op jit(solution)/shard_map/ppermute | solution.py:579
  57.4 4.0 %collective-permute-start.9 = (f32[64,128]{1,0:T(8,128)S(1)}, f32[64,128]{1,0:T(8,128)S(1)}, u32[]{:S(2)}, u32[]{:S(2)}) collective-permute-start(f32[64,128]{1,0:T(8,128)S(1)} %multiply_add_fusion.1.refs_3_), channel_id=1, source_target_pairs={{0,96},{32,0},{64,32},{96,64},{1,97},{33,1},{65,33},{97,65},{2,98}... | collective-permute-start | bytes 98312 | tf_op jit(solution)/shard_map/ppermute | solution.py:579
  57.5 5.4 %collective-permute-start.8 = (f32[64,128]{1,0:T(8,128)S(1)}, f32[64,128]{1,0:T(8,128)S(1)}, u32[]{:S(2)}, u32[]{:S(2)}) collective-permute-start(f32[64,128]{1,0:T(8,128)S(1)} %multiply_add_fusion.1.refs_3_), channel_id=1, source_target_pairs={{0,64},{32,96},{64,0},{96,32},{1,65},{33,97},{65,1},{97,33},{2,66}... | collective-permute-start | bytes 98312 | tf_op jit(solution)/shard_map/ppermute | solution.py:579
  59.7 5.1 %collective-permute-start.7 = (f32[64,128]{1,0:T(8,128)S(1)}, f32[64,128]{1,0:T(8,128)S(1)}, u32[]{:S(2)}, u32[]{:S(2)}) collective-permute-start(f32[64,128]{1,0:T(8,128)S(1)} %multiply_add_fusion.1.refs_3_), channel_id=1, source_target_pairs={{0,32},{32,64},{64,96},{96,0},{1,33},{33,65},{65,97},{97,1},{2,34}... | collective-permute-start | bytes 98312 | tf_op jit(solution)/shard_map/ppermute | solution.py:579
  87.7 1.3 %collective-permute-start.11 = (f32[64,128]{1,0:T(8,128)S(1)}, f32[64,128]{1,0:T(8,128)S(1)}, u32[]{:S(2)}, u32[]{:S(2)}) collective-permute-start(f32[64,128]{1,0:T(8,128)S(1)} %bitcast.58), channel_id=1, source_target_pairs={{0,1},{1,0},{2,3},{3,2},{4,5},{5,4},{6,7},{7,6},{8,9},{9,8},{10,11... | collective-permute-start | bytes 98312 | tf_op jit(solution)/shard_map/ppermute | solution.py:579
  89.0 4.0 %collective-permute-start.14 = (f32[64,128]{1,0:T(8,128)S(1)}, f32[64,128]{1,0:T(8,128)S(1)}, u32[]{:S(2)}, u32[]{:S(2)}) collective-permute-start(f32[64,128]{1,0:T(8,128)S(1)} %multiply_add_fusion.refs_3_), channel_id=1, source_target_pairs={{0,96},{32,0},{64,32},{96,64},{1,97},{33,1},{65,33},{97,65},{2,98}... | collective-permute-start | bytes 98312 | tf_op jit(solution)/shard_map/ppermute | solution.py:579
  89.3 5.5 %collective-permute-start.13 = (f32[64,128]{1,0:T(8,128)S(1)}, f32[64,128]{1,0:T(8,128)S(1)}, u32[]{:S(2)}, u32[]{:S(2)}) collective-permute-start(f32[64,128]{1,0:T(8,128)S(1)} %multiply_add_fusion.refs_3_), channel_id=1, source_target_pairs={{0,64},{32,96},{64,0},{96,32},{1,65},{33,97},{65,1},{97,33},{2,66}... | collective-permute-start | bytes 98312 | tf_op jit(solution)/shard_map/ppermute | solution.py:579
  90.4 5.3 %collective-permute-start.12 = (f32[64,128]{1,0:T(8,128)S(1)}, f32[64,128]{1,0:T(8,128)S(1)}, u32[]{:S(2)}, u32[]{:S(2)}) collective-permute-start(f32[64,128]{1,0:T(8,128)S(1)} %multiply_add_fusion.refs_3_), channel_id=1, source_target_pairs={{0,32},{32,64},{64,96},{96,0},{1,33},{33,65},{65,97},{97,1},{2,34}... | collective-permute-start | bytes 98312 | tf_op jit(solution)/shard_map/ppermute | solution.py:579
  115.6 11.7 %copy-start = (f32[4096]{0:T(1024)S(1)}, f32[4096]{0:T(1024)}, u32[]{:S(2)}) copy-start(f32[4096]{0:T(1024)} %param.11) | copy-start | bytes 49156
  115.6 11.7 %copy-start.3 = (s32[4,8]{1,0:T(4,128)S(1)}, s32[4,8]{1,0:T(4,128)}, u32[]{:S(2)}) copy-start(s32[4,8]{1,0:T(4,128)} %refs_4_) | copy-start | bytes 388
  115.6 11.7 %copy-start.4 = (f32[32,128]{1,0:T(8,128)S(1)}, f32[32,128]{1,0:T(8,128)}, u32[]{:S(2)}) copy-start(f32[32,128]{1,0:T(8,128)} %get-tuple-element.87.refs_9_) | copy-start | bytes 49156
  119.5 1.3 collective-permute-start.16
  119.7 3.4 %collective-permute-start.15 = (f32[32,128]{1,0:T(8,128)S(1)}, f32[32,128]{1,0:T(8,128)S(1)}, u32[]{:S(2)}, u32[]{:S(2)}) collective-permute-start(f32[32,128]{1,0:T(8,128)S(1)} %multiply_add_fusion.2), channel_id=1, source_target_pairs={{0,1},{1,0},{2,3},{3,2},{4,5},{5,4},{6,7},{7,6},{8,9},{9,8},{10,11... | collective-permute-start | bytes 49160 | tf_op jit(solution)/shard_map/ppermute | solution.py:579
  120.9 3.7 %collective-permute-start.19 = (f32[8,128]{1,0:T(8,128)S(1)}, f32[8,128]{1,0:T(8,128)S(1)}, u32[]{:S(2)}, u32[]{:S(2)}) collective-permute-start(f32[8,128]{1,0:T(8,128)S(1)} %get-tuple-element.94), channel_id=1, source_target_pairs={{0,96},{32,0},{64,32},{96,64},{1,97},{33,1},{65,33},{97,65},{2,98}... | collective-permute-start | bytes 12296 | tf_op jit(solution)/shard_map/ppermute | solution.py:656
  121.0 5.2 %collective-permute-start.18 = (f32[8,128]{1,0:T(8,128)S(1)}, f32[8,128]{1,0:T(8,128)S(1)}, u32[]{:S(2)}, u32[]{:S(2)}) collective-permute-start(f32[8,128]{1,0:T(8,128)S(1)} %get-tuple-element.95), channel_id=1, source_target_pairs={{0,64},{32,96},{64,0},{96,32},{1,65},{33,97},{65,1},{97,33},{2,66}... | collective-permute-start | bytes 12296 | tf_op jit(solution)/shard_map/ppermute | solution.py:656
  121.8 5.5 %collective-permute-start.17 = (f32[8,128]{1,0:T(8,128)S(1)}, f32[8,128]{1,0:T(8,128)S(1)}, u32[]{:S(2)}, u32[]{:S(2)}) collective-permute-start(f32[8,128]{1,0:T(8,128)S(1)} %get-tuple-element.96), channel_id=1, source_target_pairs={{0,32},{32,64},{64,96},{96,0},{1,33},{33,65},{65,97},{97,1},{2,34}... | collective-permute-start | bytes 12296 | tf_op jit(solution)/shard_map/ppermute | solution.py:656

commit v2 on v1

--- a/solution.py
+++ b/solution.py
@@ -248,6 +248,7 @@
             rows += [part.astype(jnp.float32) for part in split3(start) + split3(mass)]
             out_ref[other, c * D : (c + 1) * D, :] = block
         out_ref[other, per_peer * D :, :] = jnp.concatenate(rows, axis=0).astype(jnp.bfloat16)
+    norm_ref[...] += EPSILON * logmass[...]
 
 
 def pack(place, ids, *values):
@@ -264,27 +265,26 @@
     )(place.reshape(1), *remotes)
 
 
-def merge_kernel(peers, place_ref, *refs):
-    sums, ids, (logmass_ref, norm_ref, out_ref, parts) = refs[:peers], refs[peers : 2 * peers], refs[2 * peers :]
-    place = place_ref[0]
+def merge_kernel(wanted_ref, *refs):
+    *sums, base_ref, out_ref, parts = refs
+    per_peer = sums[0].shape[0]
     parts[...] = jnp.full_like(parts, LOWEST)
-    for d in range(peers):
-        for c in range(sums[d].shape[0]):
-            parts[d, pl.ds(ids[d][place, c], 1), :] = sums[d][c : c + 1, :]
-    merged = log_sum([parts[d] for d in range(peers)])
-    out_ref[...] = (LOG2E * logmass_ref[...] - merged) * (1.0 / SCALE) + norm_ref[...]
-
-
-def merge(place, sums, ids, logmass, norm):
-    peers = len(ids)
+    for d, sums_ref in enumerate(sums):
+        for c in range(per_peer):
+            parts[d, pl.ds(wanted_ref[d * per_peer + c], 1), :] = sums_ref[c : c + 1, :]
+    merged = log_sum([parts[d] for d in range(len(sums))])
+    out_ref[...] = base_ref[...] - (1.0 / SCALE) * merged
+
+
+def merge(wanted, sums, base):
     return pl.pallas_call(
-        functools.partial(merge_kernel, peers),
-        out_shape=shape(norm.shape),
-        in_specs=[SMEM] + [VMEM] * peers + [SMEM] * peers + [VMEM] * 2,
+        merge_kernel,
+        out_shape=shape(base.shape),
+        in_specs=[SMEM] + [VMEM] * (len(sums) + 1),
         out_specs=VMEM,
-        scratch_shapes=[pltpu.VMEM((peers, *norm.shape), jnp.float32)],
+        scratch_shapes=[pltpu.VMEM((len(sums), *base.shape), jnp.float32)],
         compiler_params=PASS,
-    )(place.reshape(1), *sums, *ids, logmass, norm)
+    )(wanted, *sums, base)
 
 
 def scaled_block(points, b):
@@ -295,9 +295,10 @@
     return wide, jnp.concatenate([high, low], axis=0)
 
 
-def source_kernel(half_ref, points_hbm, logmass_hbm, *refs):
-    count = (len(refs) - 8) // 2
-    ids_hbm, (blocks_hbm, norm_ref, same_ref, points, logmass, blocks, rows, *ids, sems) = refs[:count], refs[count:]
+def source_kernel(half_ref, place_ref, points_hbm, logmass_hbm, *refs):
+    count = (len(refs) - 9) // 2
+    ids_hbm, (blocks_hbm, norm_ref, same_ref, wanted_ref, *locals_) = refs[:count], refs[count:]
+    points, logmass, blocks, rows, *ids, sems = locals_
     halves = blocks.shape[1] - 1
     own = pl.ds(pl.multiple_of(half_ref[0] * halves, halves), halves)
     at = pl.multiple_of(half_ref[0] * (halves * BLOCK), halves * BLOCK)
@@ -324,11 +325,15 @@
         copies.append(pltpu.make_async_copy(blocks.at[own], blocks_hbm.at[own], sems.at[2 + count + k]))
         copies[-1].start()
     same_targets(ids, rows, same_ref)
+    peers, per_peer = ids[0].shape
+    for d in range(peers):
+        for c in range(per_peer):
+            wanted_ref[d * per_peer + c] = ids[d][place_ref[0], c]
     for copy in copies:
         copy.wait()
 
 
-def source(half, halves, points, logmass, ids):
+def source(half, place, halves, points, logmass, ids):
     blocks = (2, halves + 1, BLOCK, BLOCK)
     return pl.pallas_call(
         source_kernel,
@@ -336,9 +341,10 @@
             shape(blocks, jnp.bfloat16),
             shape((halves, BLOCK)),
             shape((BLOCK, BLOCK), jnp.bfloat16),
+            shape((GROUP,), jnp.int32),
         ],
-        in_specs=[SMEM] + [HBM] * (2 + len(ids)),
-        out_specs=[HBM, VMEM, VMEM],
+        in_specs=[SMEM] * 2 + [HBM] * (2 + len(ids)),
+        out_specs=[HBM, VMEM, VMEM, SMEM],
         scratch_shapes=[
             pltpu.VMEM((D, halves * BLOCK), jnp.bfloat16),
             pltpu.VMEM((halves, BLOCK), jnp.float32),
@@ -348,7 +354,7 @@
         + [pltpu.SMEM(value.shape, value.dtype) for value in ids]
         + [pltpu.SemaphoreType.DMA((2 + len(ids) + PARTS,))],
         compiler_params=PASS,
-    )(half.reshape(1), points, logmass, *ids)
+    )(half.reshape(1), place.reshape(1), points, logmass, *ids)
 
 
 def field_bias(mass_ref, parts_ref):
@@ -605,7 +611,7 @@
     tiles = [tile_slot.T, tile_counts.T]
     ids = ring(fetch_ids, "src", peers)
     ids, tiles = lax.optimization_barrier((ids, tiles + [swap(part) for part in tiles]))
-    packed, target_half = pack(
+    packed, target_base = pack(
         place,
         ids,
         target_points.T,
@@ -625,7 +631,8 @@
             turned = source_points.T
             rows, targets = log_sums(FIRST, row_pairs, halves, [*both, turned], [half.reshape(1)], groups // 2)
             rows, turned, logmass, ids = lax.optimization_barrier((rows, turned, source_logmass, ids))
-            points, source_half, same = source(half, halves, turned, logmass.reshape(blocks, BLOCK), ids)
+            logmass = logmass.reshape(blocks, BLOCK)
+            points, source_half, same, wanted = source(half, place, halves, turned, logmass, ids)
             same = [same, swap(same)]
         else:
             (rows,) = log_sums(ROWS, row_pairs, halves, [targets, points], col_parts + same, groups // 2)
@@ -646,15 +653,13 @@
     source_field = jnp.concatenate([jnp.where(low, field, other), jnp.where(low, other, field)], axis=0)
 
     cols = log_sum([cols[:count], swap(cols[count:])]).reshape(peers, per_peer, BLOCK)
-    cols, last_place, ids, target_half, target_logmass = lax.optimization_barrier(
-        (cols, place, ids, target_half, target_logmass)
-    )
+    cols, last_place, wanted, target_base = lax.optimization_barrier((cols, place, wanted, target_base))
     back = []
     for d in range(peers):
-        wanted = lax.dynamic_slice(cols, ((last_place + d) % peers, 0, 0), (1, per_peer, BLOCK))[0]
+        part = lax.dynamic_slice(cols, ((last_place + d) % peers, 0, 0), (1, per_peer, BLOCK))[0]
         pairs = [(i, (i + d) % peers) for i in range(peers)]
-        back.append(wanted if d == 0 else lax.ppermute(wanted, "src", pairs))
-    target_field = merge(last_place, back, ids, target_logmass.reshape(owned, BLOCK), target_half).reshape(-1)
+        back.append(part if d == 0 else lax.ppermute(part, "src", pairs))
+    target_field = merge(wanted, back, target_base).reshape(-1)
     return (source_field.reshape(-1), target_field)
 
 

time: 130 us -> 129 us (level)
  starting transfers between devices: 30.6 us -> 28.1 us
  waiting for transfers between devices: 24.2 us -> 25.6 us
    ppermute x17, starting transfers between devices: 14 us -> 11.9 us  [ring(): out.append(lax.ppermute(values, axis, pairs))]
    ppermute x17, waiting for transfers between devices: 14.5 us -> 15.9 us  [ring(): out.append(lax.ppermute(values, axis, pairs))]
where the time goes in v2:
time: 129 us; the launch traced here: 127 us
  Pallas kernels  39.6 us (31%)
  blocking collectives  30.7 us (24%)
  starting transfers between devices  28.1 us (22%)
  waiting for transfers between devices  25.6 us (20%)
  local copies, waits for them, and re-layouts  1.46 us (1%)
    all_to_all x2, blocking collectives, shards(): lax.all_to_all(rows, 'grp', split_axis=0, concat_axis=0, tiled=True, axis...  30.7 us
    pallas_call x6, Pallas kernels, log_sums(): pl.pallas_call(functools.partial(pass_kernel, kind), out_shape=outs, in_s...  24.2 us
    ppermute x17, waiting for transfers between devices, ring(): out.append(lax.ppermute(values, axis, pairs))  15.9 us
    ppermute x17, starting transfers between devices, ring(): out.append(lax.ppermute(values, axis, pairs))  11.9 us
    all_to_all x1, starting transfers between devices, shards(): lax.all_to_all(rows, 'grp', split_axis=0, concat_axis=0, tiled=True, axis...  9.56 us
    pallas_call x2, Pallas kernels, make_list(): pl.pallas_call(kernel, out_shape=shape((LONG,), jnp.int32), in_specs=[SME...  8.49 us
    all_to_all x1, waiting for transfers between devices, shards(): lax.all_to_all(rows, 'grp', split_axis=0, concat_axis=0, tiled=True, axis...  4.74 us
    all_to_all x1, starting transfers between devices, shards(): lax.all_to_all(packed, 'src', split_axis=0, concat_axis=0, tiled=True)  4.51 us
  transfers between devices with their start and end apart: 22, of which 16 were waited for; matrix products, arithmetic and copies ran while one was open for 1% of the time, Pallas kernels for 9%

profile of v2, /device:TPU:0, one launch (start us, length us, event | category | flops | bytes accessed | tf_op | source)
XLA Modules:
  0.0 127.1 jit_solution(847664631104134995)
XLA Ops:
  0.6 0.1 collective-permute-start.3
  0.7 3.2 %collective-permute-start.1 = (s32[4,8]{1,0:T(4,128)}, s32[4,8]{1,0:T(4,128)}, u32[]{:S(2)}, u32[]{:S(2)}) collective-permute-start(s32[4,8]{1,0:T(4,128)} %refs_0_.1), channel_id=1, source_target_pairs={{0,64},{32,96},{64,0},{96,32},{1,65},{33,97},{65,1},{97,33},{2,66}... | collective-permute-start | bytes 392 | tf_op jit(solution)/shard_map/ppermute | solution.py:585
  3.9 0.6 collective-permute-start
  4.5 2.6 %collective-permute-start.2 = (s32[4,8]{1,0:T(4,128)}, s32[4,8]{1,0:T(4,128)}, u32[]{:S(2)}, u32[]{:S(2)}) collective-permute-start(s32[4,8]{1,0:T(4,128)} %refs_0_.1), channel_id=1, source_target_pairs={{0,96},{32,0},{64,32},{96,64},{1,97},{33,1},{65,33},{97,65},{2,98}... | collective-permute-start | bytes 392 | tf_op jit(solution)/shard_map/ppermute | solution.py:585
  7.2 1.9 %collective-permute-done.refs_1_ = s32[4,8]{1,0:T(4,128)} collective-permute-done((s32[4,8]{1,0:T(4,128)}, s32[4,8]{1,0:T(4,128)}, u32[]{:S(2)}, u32[]{:S(2)}) %collective-permute-start) | collective-permute-done | bytes 160 | tf_op jit(solution)/shard_map/ppermute | solution.py:585
  9.0 2.4 %shard_map.95 = (bf16[4,560,128]{2,1,0:T(8,128)(2,1)}, f32[32,128]{1,0:T(8,128)}) custom-call(s32[1]{0:T(128)} %bitcast.place_ref, s32[4,8]{1,0:T(4,128)} %refs_0_.1, s32[4,8]{1,0:T(4,128)} %collective-permute-done.refs_1_, s32[4,8]{1,0:T(4,128)} %collective-permute-done.1.refs_2_, s32[4,8]{1,0:T(4,128)} %collective-permute-done.2.refs_3_, ...), custom_call_target="tpu_custom_call" | custom-call | tf_op jit(solution)/shard_map/pallas_call | solution.py:256
  11.4 4.5 %all-to-all-start = ((bf16[4,560,128]{2,1,0:T(8,128)(2,1)}), bf16[4,560,128]{2,1,0:T(8,128)(2,1)}, u32[]{:S(2)}, u32[]{:S(2)}) async-start(bf16[4,560,128]{2,1,0:T(8,128)(2,1)} %get-tuple-element.46), calls=%async_computation | async-start | bytes 1146880 | tf_op jit(solution)/shard_map/all_to_all | solution.py:623
  15.9 2.8 %shard_map.97.refs_0_ = s32[1048576]{0:T(1024)} custom-call(s32[1]{0:T(128)} %bitcast.6.half_ref.refs_4_, s32[8,64]{1,0:T(8,128)} %bitcast.62, s32[1,64]{1,0:T(1,128)} %bitcast.68, s32[8,64]{1,0:T(8,128)} %collective-permute-done.3.refs_2_, s32[1,64]{1,0:T(1,128)} %collective-permute-done.4.refs_3_), custom_call_target="tpu_custom_call" | custom-call | tf_op jit(solution)/shard_map/pallas_call | solution.py:196
  18.7 5.7 %shard_map.96.refs_0_ = s32[1048576]{0:T(1024)} custom-call(s32[1]{0:T(128)} %bitcast.6.half_ref.refs_4_, s32[8,64]{1,0:T(8,128)} %bitcast.63, s32[1,64]{1,0:T(1,128)} %bitcast.69, s32[8,64]{1,0:T(8,128)} %collective-permute-done.3.refs_2_, s32[1,64]{1,0:T(1,128)} %collective-permute-done.4.refs_3_), custom_call_target="tpu_custom_call" | custom-call | tf_op jit(solution)/shard_map/pallas_call | solution.py:196
  24.4 1.4 %all-to-all-done.refs_1_ = bf16[4,560,128]{2,1,0:T(8,128)(2,1)} async-done(((bf16[4,560,128]{2,1,0:T(8,128)(2,1)}), bf16[4,560,128]{2,1,0:T(8,128)(2,1)}, u32[]{:S(2)}, u32[]{:S(2)}) %all-to-all-start) | async-done | bytes 573472 | tf_op jit(solution)/shard_map/all_to_all | solution.py:623
  25.8 2.3 %collective-permute-done.5.refs_2_ = bf16[4,560,128]{2,1,0:T(8,128)(2,1)} collective-permute-done((bf16[4,560,128]{2,1,0:T(8,128)(2,1)}, bf16[4,560,128]{2,1,0:T(8,128)(2,1)}, u32[]{:S(2)}, u32[]{:S(2)}) %collective-permute-start.5) | collective-permute-done | bytes 573472 | tf_op jit(solution)/shard_map/ppermute | solution.py:585
  28.1 5.4 %shard_map.98 = (f32[16,32,128]{2,1,0:T(8,128)}, bf16[66,128,128]{2,1,0:T(8,128)(2,1)}) custom-call(s32[1048576]{0:T(1024)} %shard_map.96.refs_0_, bf16[4,560,128]{2,1,0:T(8,128)(2,1)} %all-to-all-done.refs_1_, bf16[4,560,128]{2,1,0:T(8,128)(2,1)} %collective-permute-done.5.refs_2_, bf16[64,8192]{1,0:T(8,128)(2,1)} %bitcast.58, s32[1]{0:T(128)} %bitcast.6.half_ref.refs_4_), custom_call_target="tpu_custom_call" | custom-call | tf_op jit(solution)/shard_map/pallas_call | solution.py:558
  33.5 9.6 %all-to-all-start.1 = ((f32[16,32,128]{2,1,0:T(8,128)}), f32[16,32,128]{2,1,0:T(8,128)S(1)}, u32[]{:S(2)}, u32[]{:S(2)}) async-start(f32[16,32,128]{2,1,0:T(8,128)} %get-tuple-element.69), calls=%async_computation.1 | async-start | bytes 524288 | tf_op jit(solution)/shard_map/all_to_all | solution.py:639
  43.1 0.7 copy-done
  43.8 0.7 copy-done.2
  44.5 3.4 %shard_map.99 = (bf16[2,33,128,128]{3,2,1,0:T(8,128)(2,1)}, f32[32,128]{1,0:T(8,128)S(1)}, bf16[128,128]{1,0:T(8,128)(2,1)S(1)}, s32[32]{0:T(128)S(1)}) custom-call(s32[1]{0:T(128)} %bitcast.6.half_ref.refs_4_, s32[1]{0:T(128)} %bitcast.place_ref, bf16[64,8192]{1,0:T(8,128)(2,1)} %bitcast.59, f32[64,128]{1,0:T(8,128)S(1)} %bitcast.57, s32[4,8]{1,0:T(4,128)S(1)} %copy-done.2, ...), custom_call_target="tpu_custom_call" | custom-call | tf_op jit(solution)/shard_map/pallas_call | solution.py:338
  47.9 4.7 %all-to-all-done.1.refs_4_ = f32[16,32,128]{2,1,0:T(8,128)S(1)} async-done(((f32[16,32,128]{2,1,0:T(8,128)}), f32[16,32,128]{2,1,0:T(8,128)S(1)}, u32[]{:S(2)}, u32[]{:S(2)}) %all-to-all-start.1) | async-done | bytes 262176 | tf_op jit(solution)/shard_map/all_to_all | solution.py:639
  52.6 3.7 %shard_map.100 = f32[1,64,128]{2,1,0:T(8,128)S(1)} custom-call(s32[1048576]{0:T(1024)} %shard_map.97.refs_0_, bf16[4,560,128]{2,1,0:T(8,128)(2,1)} %all-to-all-done.refs_1_, bf16[4,560,128]{2,1,0:T(8,128)(2,1)} %collective-permute-done.5.refs_2_, bf16[2,33,128,128]{3,2,1,0:T(8,128)(2,1)} %get-tuple-element.67.refs_3_.refs_2_, ...), custom_call_target="tpu_custom_call" | custom-call | tf_op jit(solution)/shard_map/pallas_call | solution.py:558
  56.4 0.5 collective-permute-start.10
  56.9 0.7 collective-permute-done.6
  57.7 0.7 collective-permute-start.8
  58.5 1.3 %collective-permute-start.7 = (f32[64,128]{1,0:T(8,128)S(1)}, f32[64,128]{1,0:T(8,128)S(1)}, u32[]{:S(2)}, u32[]{:S(2)}) collective-permute-start(f32[64,128]{1,0:T(8,128)S(1)} %multiply_add_fusion.1.refs_3_), channel_id=1, source_target_pairs={{0,32},{32,64},{64,96},{96,0},{1,33},{33,65},{65,97},{97,1},{2,34}... | collective-permute-start | bytes 98312 | tf_op jit(solution)/shard_map/ppermute | solution.py:585
  59.7 1.9 %collective-permute-done.9.refs_6_ = f32[64,128]{1,0:T(8,128)S(1)} collective-permute-done((f32[64,128]{1,0:T(8,128)S(1)}, f32[64,128]{1,0:T(8,128)S(1)}, u32[]{:S(2)}, u32[]{:S(2)}) %collective-permute-start.9) | collective-permute-done | bytes 32800 | tf_op jit(solution)/shard_map/ppermute | solution.py:585
  61.6 1.7 %collective-permute-done.8.refs_5_ = f32[64,128]{1,0:T(8,128)S(1)} collective-permute-done((f32[64,128]{1,0:T(8,128)S(1)}, f32[64,128]{1,0:T(8,128)S(1)}, u32[]{:S(2)}, u32[]{:S(2)}) %collective-permute-start.8) | collective-permute-done | bytes 32800 | tf_op jit(solution)/shard_map/ppermute | solution.py:585
  63.3 1.0 collective-permute-done.7.refs_4_
  64.3 3.8 %shard_map.101 = f32[16,32,128]{2,1,0:T(8,128)S(1)} custom-call(s32[1048576]{0:T(1024)} %shard_map.96.refs_0_, bf16[66,128,128]{2,1,0:T(8,128)(2,1)} %get-tuple-element.68.refs_1_, bf16[2,33,128,128]{3,2,1,0:T(8,128)(2,1)} %get-tuple-element.67.refs_3_.refs_2_, f32[64,128]{1,0:T(8,128)S(1)} %multiply_add_fusion.1.refs_3_, ...), custom_call_target="tpu_custom_call" | custom-call | tf_op jit(solution)/shard_map/pallas_call | solution.py:558
  68.1 15.4 %all_to_all.20.refs_4_ = f32[16,32,128]{2,1,0:T(8,128)S(1)} all-to-all(f32[16,32,128]{2,1,0:T(8,128)S(1)} %shard_map.101), channel_id=1, replica_groups={{0,2,4,6,8,10,12,14,16,18,20,22,24,26,28,30},{1,3,5,7,9,11,13,15,17,19,..., dimensions={0} | all-to-all | bytes 524288 | tf_op jit(solution)/shard_map/all_to_all | solution.py:639
  83.5 3.7 %shard_map.102 = f32[1,64,128]{2,1,0:T(8,128)S(1)} custom-call(s32[1048576]{0:T(1024)} %shard_map.97.refs_0_, bf16[4,560,128]{2,1,0:T(8,128)(2,1)} %all-to-all-done.refs_1_, bf16[4,560,128]{2,1,0:T(8,128)(2,1)} %collective-permute-done.5.refs_2_, bf16[2,33,128,128]{3,2,1,0:T(8,128)(2,1)} %get-tuple-element.67.refs_3_.refs_2_, ...), custom_call_target="tpu_custom_call" | custom-call | tf_op jit(solution)/shard_map/pallas_call | solution.py:558
  87.3 1.2 collective-permute-done.11
  88.5 0.2 collective-permute-start.14
  88.7 0.9 collective-permute-start.13
  89.6 1.0 collective-permute-start.12
  90.6 1.9 %collective-permute-done.14.refs_6_ = f32[64,128]{1,0:T(8,128)S(1)} collective-permute-done((f32[64,128]{1,0:T(8,128)S(1)}, f32[64,128]{1,0:T(8,128)S(1)}, u32[]{:S(2)}, u32[]{:S(2)}) %collective-permute-start.14) | collective-permute-done | bytes 32800 | tf_op jit(solution)/shard_map/ppermute | solution.py:585
  92.5 1.7 %collective-permute-done.13.refs_5_ = f32[64,128]{1,0:T(8,128)S(1)} collective-permute-done((f32[64,128]{1,0:T(8,128)S(1)}, f32[64,128]{1,0:T(8,128)S(1)}, u32[]{:S(2)}, u32[]{:S(2)}) %collective-permute-start.13) | collective-permute-done | bytes 32800 | tf_op jit(solution)/shard_map/ppermute | solution.py:585
  94.2 0.9 collective-permute-done.12.refs_4_
  95.2 3.8 %shard_map.103 = f32[16,32,128]{2,1,0:T(8,128)S(1)} custom-call(s32[1048576]{0:T(1024)} %shard_map.96.refs_0_, bf16[66,128,128]{2,1,0:T(8,128)(2,1)} %get-tuple-element.68.refs_1_, bf16[2,33,128,128]{3,2,1,0:T(8,128)(2,1)} %get-tuple-element.67.refs_3_.refs_2_, f32[64,128]{1,0:T(8,128)S(1)} %multiply_add_fusion.refs_3_, ...), custom_call_target="tpu_custom_call" | custom-call | tf_op jit(solution)/shard_map/pallas_call | solution.py:558
  98.9 15.3 %all_to_all.21.refs_4_ = f32[16,32,128]{2,1,0:T(8,128)S(1)} all-to-all(f32[16,32,128]{2,1,0:T(8,128)S(1)} %shard_map.103), channel_id=1, replica_groups={{0,2,4,6,8,10,12,14,16,18,20,22,24,26,28,30},{1,3,5,7,9,11,13,15,17,19,..., dimensions={0} | all-to-all | bytes 524288 | tf_op jit(solution)/shard_map/all_to_all | solution.py:639
  114.2 3.9 %shard_map.104 = (f32[1,64,128]{2,1,0:T(8,128)S(1)}, f32[32,128]{1,0:T(8,128)S(1)}) custom-call(s32[1048576]{0:T(1024)} %shard_map.97.refs_0_, bf16[4,560,128]{2,1,0:T(8,128)(2,1)} %all-to-all-done.refs_1_, bf16[4,560,128]{2,1,0:T(8,128)(2,1)} %collective-permute-done.5.refs_2_, bf16[2,33,128,128]{3,2,1,0:T(8,128)(2,1)} %get-tuple-element.67.refs_3_.refs_2_, ...), custom_call_target="tpu_custom_call" | custom-call | tf_op jit(solution)/shard_map/pallas_call | solution.py:558
  118.3 0.5 collective-permute-start.15
  118.8 0.7 collective-permute-done.16
  119.5 0.3 collective-permute-start.19
  119.9 0.9 collective-permute-start.18
  120.8 0.9 collective-permute-start.17
  121.7 0.6 maximum_bitcast_fusion
  122.3 0.9 collective-permute-done.19.refs_3_
  123.2 1.7 %collective-permute-done.18.refs_2_ = f32[8,128]{1,0:T(8,128)S(1)} collective-permute-done((f32[8,128]{1,0:T(8,128)S(1)}, f32[8,128]{1,0:T(8,128)S(1)}, u32[]{:S(2)}, u32[]{:S(2)}) %collective-permute-start.18) | collective-permute-done | bytes 4128 | tf_op jit(solution)/shard_map/ppermute | solution.py:661
  125.0 0.9 collective-permute-done.17.refs_1_
  125.9 1.2 shard_map.105
  (25 shorter events, 0.5 us)
Async XLA Ops:
  0.6 8.4 %collective-permute-start.3 = (s32[8,64]{1,0:T(8,128)}, s32[8,64]{1,0:T(8,128)}, u32[]{:S(2)}, u32[]{:S(2)}) collective-permute-start(s32[8,64]{1,0:T(8,128)} %bitcast.61), channel_id=1, source_target_pairs={{0,1},{1,0},{2,3},{3,2},{4,5},{5,4},{6,7},{7,6},{8,9},{9,8},{10,11... | collective-permute-start | bytes 6152 | tf_op jit(solution)/shard_map/ppermute | solution.py:585
  0.7 6.4 %collective-permute-start.1 = (s32[4,8]{1,0:T(4,128)}, s32[4,8]{1,0:T(4,128)}, u32[]{:S(2)}, u32[]{:S(2)}) collective-permute-start(s32[4,8]{1,0:T(4,128)} %refs_0_.1), channel_id=1, source_target_pairs={{0,64},{32,96},{64,0},{96,32},{1,65},{33,97},{65,1},{97,33},{2,66}... | collective-permute-start | bytes 392 | tf_op jit(solution)/shard_map/ppermute | solution.py:585
  3.9 5.1 %collective-permute-start = (s32[4,8]{1,0:T(4,128)}, s32[4,8]{1,0:T(4,128)}, u32[]{:S(2)}, u32[]{:S(2)}) collective-permute-start(s32[4,8]{1,0:T(4,128)} %refs_0_.1), channel_id=1, source_target_pairs={{0,32},{32,64},{64,96},{96,0},{1,33},{33,65},{65,97},{97,1},{2,34}... | collective-permute-start | bytes 392 | tf_op jit(solution)/shard_map/ppermute | solution.py:585
  4.5 4.5 %collective-permute-start.2 = (s32[4,8]{1,0:T(4,128)}, s32[4,8]{1,0:T(4,128)}, u32[]{:S(2)}, u32[]{:S(2)}) collective-permute-start(s32[4,8]{1,0:T(4,128)} %refs_0_.1), channel_id=1, source_target_pairs={{0,96},{32,0},{64,32},{96,64},{1,97},{33,1},{65,33},{97,65},{2,98}... | collective-permute-start | bytes 392 | tf_op jit(solution)/shard_map/ppermute | solution.py:585
  7.2 1.9 %collective-permute-start.4 = (s32[1,64]{1,0:T(1,128)}, s32[1,64]{1,0:T(1,128)}, u32[]{:S(2)}, u32[]{:S(2)}) collective-permute-start(s32[1,64]{1,0:T(1,128)} %bitcast.67), channel_id=1, source_target_pairs={{0,1},{1,0},{2,3},{3,2},{4,5},{5,4},{6,7},{7,6},{8,9},{9,8},{10,11... | collective-permute-start | bytes 776 | tf_op jit(solution)/shard_map/ppermute | solution.py:585
  11.4 14.4 %all-to-all-start = ((bf16[4,560,128]{2,1,0:T(8,128)(2,1)}), bf16[4,560,128]{2,1,0:T(8,128)(2,1)}, u32[]{:S(2)}, u32[]{:S(2)}) async-start(bf16[4,560,128]{2,1,0:T(8,128)(2,1)} %get-tuple-element.46), calls=%async_computation | async-start | bytes 1146880 | tf_op jit(solution)/shard_map/all_to_all | solution.py:623
  25.8 2.3 %collective-permute-start.5 = (bf16[4,560,128]{2,1,0:T(8,128)(2,1)}, bf16[4,560,128]{2,1,0:T(8,128)(2,1)}, u32[]{:S(2)}, u32[]{:S(2)}) collective-permute-start(bf16[4,560,128]{2,1,0:T(8,128)(2,1)} %all-to-all-done.refs_1_), channel_id=1, source_target_pairs={{0,1},{1,0},{2,3},{3,2},{4,5},{5,4},{6,7},{7,6},{8,9},{9,8},{10,11... | collective-permute-start | bytes 1720328 | tf_op jit(solution)/shard_map/ppermute | solution.py:585
  33.5 19.1 %all-to-all-start.1 = ((f32[16,32,128]{2,1,0:T(8,128)}), f32[16,32,128]{2,1,0:T(8,128)S(1)}, u32[]{:S(2)}, u32[]{:S(2)}) async-start(f32[16,32,128]{2,1,0:T(8,128)} %get-tuple-element.69), calls=%async_computation.1 | async-start | bytes 524288 | tf_op jit(solution)/shard_map/all_to_all | solution.py:639
  43.1 0.8 copy-start
  43.8 0.7 copy-start.2
  56.3 1.3 %collective-permute-start.6 = (f32[64,128]{1,0:T(8,128)S(1)}, f32[64,128]{1,0:T(8,128)S(1)}, u32[]{:S(2)}, u32[]{:S(2)}) collective-permute-start(f32[64,128]{1,0:T(8,128)S(1)} %bitcast.55), channel_id=1, source_target_pairs={{0,1},{1,0},{2,3},{3,2},{4,5},{5,4},{6,7},{7,6},{8,9},{9,8},{10,11... | collective-permute-start | bytes 98312 | tf_op jit(solution)/shard_map/ppermute | solution.py:585
  56.4 3.3 %collective-permute-start.10 = (bf16[128,128]{1,0:T(8,128)(2,1)S(1)}, bf16[128,128]{1,0:T(8,128)(2,1)S(1)}, u32[]{:S(2)}, u32[]{:S(2)}) collective-permute-start(bf16[128,128]{1,0:T(8,128)(2,1)S(1)} %get-tuple-element.70.refs_7_), channel_id=1, source_target_pairs={{0,1},{1,0},{2,3},{3,2},{4,5},{5,4},{6,7},{7,6},{8,9},{9,8},{10,11... | collective-permute-start | bytes 98312 | tf_op jit(solution)/shard_map/ppermute | solution.py:585
  57.6 4.0 %collective-permute-start.9 = (f32[64,128]{1,0:T(8,128)S(1)}, f32[64,128]{1,0:T(8,128)S(1)}, u32[]{:S(2)}, u32[]{:S(2)}) collective-permute-start(f32[64,128]{1,0:T(8,128)S(1)} %multiply_add_fusion.1.refs_3_), channel_id=1, source_target_pairs={{0,96},{32,0},{64,32},{96,64},{1,97},{33,1},{65,33},{97,65},{2,98}... | collective-permute-start | bytes 98312 | tf_op jit(solution)/shard_map/ppermute | solution.py:585
  57.7 5.6 %collective-permute-start.8 = (f32[64,128]{1,0:T(8,128)S(1)}, f32[64,128]{1,0:T(8,128)S(1)}, u32[]{:S(2)}, u32[]{:S(2)}) collective-permute-start(f32[64,128]{1,0:T(8,128)S(1)} %multiply_add_fusion.1.refs_3_), channel_id=1, source_target_pairs={{0,64},{32,96},{64,0},{96,32},{1,65},{33,97},{65,1},{97,33},{2,66}... | collective-permute-start | bytes 98312 | tf_op jit(solution)/shard_map/ppermute | solution.py:585
  58.5 5.9 %collective-permute-start.7 = (f32[64,128]{1,0:T(8,128)S(1)}, f32[64,128]{1,0:T(8,128)S(1)}, u32[]{:S(2)}, u32[]{:S(2)}) collective-permute-start(f32[64,128]{1,0:T(8,128)S(1)} %multiply_add_fusion.1.refs_3_), channel_id=1, source_target_pairs={{0,32},{32,64},{64,96},{96,0},{1,33},{33,65},{65,97},{97,1},{2,34}... | collective-permute-start | bytes 98312 | tf_op jit(solution)/shard_map/ppermute | solution.py:585
  87.2 1.3 %collective-permute-start.11 = (f32[64,128]{1,0:T(8,128)S(1)}, f32[64,128]{1,0:T(8,128)S(1)}, u32[]{:S(2)}, u32[]{:S(2)}) collective-permute-start(f32[64,128]{1,0:T(8,128)S(1)} %bitcast.56), channel_id=1, source_target_pairs={{0,1},{1,0},{2,3},{3,2},{4,5},{5,4},{6,7},{7,6},{8,9},{9,8},{10,11... | collective-permute-start | bytes 98312 | tf_op jit(solution)/shard_map/ppermute | solution.py:585
  88.5 4.0 %collective-permute-start.14 = (f32[64,128]{1,0:T(8,128)S(1)}, f32[64,128]{1,0:T(8,128)S(1)}, u32[]{:S(2)}, u32[]{:S(2)}) collective-permute-start(f32[64,128]{1,0:T(8,128)S(1)} %multiply_add_fusion.refs_3_), channel_id=1, source_target_pairs={{0,96},{32,0},{64,32},{96,64},{1,97},{33,1},{65,33},{97,65},{2,98}... | collective-permute-start | bytes 98312 | tf_op jit(solution)/shard_map/ppermute | solution.py:585
  88.7 5.5 %collective-permute-start.13 = (f32[64,128]{1,0:T(8,128)S(1)}, f32[64,128]{1,0:T(8,128)S(1)}, u32[]{:S(2)}, u32[]{:S(2)}) collective-permute-start(f32[64,128]{1,0:T(8,128)S(1)} %multiply_add_fusion.refs_3_), channel_id=1, source_target_pairs={{0,64},{32,96},{64,0},{96,32},{1,65},{33,97},{65,1},{97,33},{2,66}... | collective-permute-start | bytes 98312 | tf_op jit(solution)/shard_map/ppermute | solution.py:585
  89.6 5.6 %collective-permute-start.12 = (f32[64,128]{1,0:T(8,128)S(1)}, f32[64,128]{1,0:T(8,128)S(1)}, u32[]{:S(2)}, u32[]{:S(2)}) collective-permute-start(f32[64,128]{1,0:T(8,128)S(1)} %multiply_add_fusion.refs_3_), channel_id=1, source_target_pairs={{0,32},{32,64},{64,96},{96,0},{1,33},{33,65},{65,97},{97,1},{2,34}... | collective-permute-start | bytes 98312 | tf_op jit(solution)/shard_map/ppermute | solution.py:585
  114.2 11.7 %copy-start.1 = (f32[32,128]{1,0:T(8,128)S(1)}, f32[32,128]{1,0:T(8,128)}, u32[]{:S(2)}) copy-start(f32[32,128]{1,0:T(8,128)} %get-tuple-element.81.refs_4_) | copy-start | bytes 49156
  118.2 1.3 collective-permute-start.16
  118.3 3.4 %collective-permute-start.15 = (f32[32,128]{1,0:T(8,128)S(1)}, f32[32,128]{1,0:T(8,128)S(1)}, u32[]{:S(2)}, u32[]{:S(2)}) collective-permute-start(f32[32,128]{1,0:T(8,128)S(1)} %multiply_add_fusion.2), channel_id=1, source_target_pairs={{0,1},{1,0},{2,3},{3,2},{4,5},{5,4},{6,7},{7,6},{8,9},{9,8},{10,11... | collective-permute-start | bytes 49160 | tf_op jit(solution)/shard_map/ppermute | solution.py:585
  119.5 3.7 %collective-permute-start.19 = (f32[8,128]{1,0:T(8,128)S(1)}, f32[8,128]{1,0:T(8,128)S(1)}, u32[]{:S(2)}, u32[]{:S(2)}) collective-permute-start(f32[8,128]{1,0:T(8,128)S(1)} %get-tuple-element.88), channel_id=1, source_target_pairs={{0,96},{32,0},{64,32},{96,64},{1,97},{33,1},{65,33},{97,65},{2,98}... | collective-permute-start | bytes 12296 | tf_op jit(solution)/shard_map/ppermute | solution.py:661
  119.9 5.1 %collective-permute-start.18 = (f32[8,128]{1,0:T(8,128)S(1)}, f32[8,128]{1,0:T(8,128)S(1)}, u32[]{:S(2)}, u32[]{:S(2)}) collective-permute-start(f32[8,128]{1,0:T(8,128)S(1)} %get-tuple-element.89), channel_id=1, source_target_pairs={{0,64},{32,96},{64,0},{96,32},{1,65},{33,97},{65,1},{97,33},{2,66}... | collective-permute-start | bytes 12296 | tf_op jit(solution)/shard_map/ppermute | solution.py:661
  120.8 5.2 %collective-permute-start.17 = (f32[8,128]{1,0:T(8,128)S(1)}, f32[8,128]{1,0:T(8,128)S(1)}, u32[]{:S(2)}, u32[]{:S(2)}) collective-permute-start(f32[8,128]{1,0:T(8,128)S(1)} %get-tuple-element.90), channel_id=1, source_target_pairs={{0,32},{32,64},{64,96},{96,0},{1,33},{33,65},{65,97},{97,1},{2,34}... | collective-permute-start | bytes 12296 | tf_op jit(solution)/shard_map/ppermute | solution.py:661

commit v3 on v2

--- a/solution.py
+++ b/solution.py
@@ -391,7 +391,7 @@
             mass_ref[pl.ds(q, 1), :] = mass[0] + mass[1] + mass[2]
         return carry
 
-    lax.fori_loop(first, stop, one_peer, 0)
+    lax.fori_loop(first, stop, one_peer, 0, unroll=True)
 
 
 def pass_kernel(kind, *refs):

time: 129 us -> 132 us (1.023); the launches traced: 127 us -> 133 us
  starting transfers between devices: 28.1 us -> 37.7 us
  waiting for transfers between devices: 25.6 us -> 23.9 us
    ppermute x17, starting transfers between devices: 11.9 us -> 17.7 us  [ring(): out.append(lax.ppermute(values, axis, pairs))]
    ppermute x3, starting transfers between devices: 2.1 us -> 5.87 us  [shards(): back.append(part if d == 0 else lax.ppermute(part, 'src', pairs))]
  transfers between devices with their start and end apart: 22 -> 22, of which waited for: 16 -> 12; matrix products, arithmetic and copies ran while one was open for 1% -> 1% of each run, Pallas kernels for 9% -> 9%
where the time goes in v3:
time: 132 us; the launch traced here: 133 us
  Pallas kernels  39.2 us (30%)
  starting transfers between devices  37.7 us (29%)
  blocking collectives  29.5 us (22%)
  waiting for transfers between devices  23.9 us (18%)
  local copies, waits for them, and re-layouts  1.46 us (1%)
    all_to_all x2, blocking collectives, shards(): lax.all_to_all(rows, 'grp', split_axis=0, concat_axis=0, tiled=True, axis...  29.5 us
    pallas_call x6, Pallas kernels, log_sums(): pl.pallas_call(functools.partial(pass_kernel, kind), out_shape=outs, in_s...  23.8 us
    ppermute x17, starting transfers between devices, ring(): out.append(lax.ppermute(values, axis, pairs))  17.7 us
    ppermute x17, waiting for transfers between devices, ring(): out.append(lax.ppermute(values, axis, pairs))  15 us
    all_to_all x1, starting transfers between devices, shards(): lax.all_to_all(rows, 'grp', split_axis=0, concat_axis=0, tiled=True, axis...  9.57 us
    pallas_call x2, Pallas kernels, make_list(): pl.pallas_call(kernel, out_shape=shape((LONG,), jnp.int32), in_specs=[SME...  8.49 us
    ppermute x3, starting transfers between devices, shards(): back.append(part if d == 0 else lax.ppermute(part, 'src', pairs))  5.87 us
    all_to_all x1, waiting for transfers between devices, shards(): lax.all_to_all(rows, 'grp', split_axis=0, concat_axis=0, tiled=True, axis...  4.75 us
  transfers between devices with their start and end apart: 22, of which 12 were waited for; matrix products, arithmetic and copies ran while one was open for 1% of the time, Pallas kernels for 9%

profile of v3, /device:TPU:0, one launch (start us, length us, event | category | flops | bytes accessed | tf_op | source)
XLA Modules:
  0.0 133.4 jit_solution(17951570764424077651)
XLA Ops:
  0.6 0.1 collective-permute-start.3
  0.7 3.2 %collective-permute-start.1 = (s32[4,8]{1,0:T(4,128)}, s32[4,8]{1,0:T(4,128)}, u32[]{:S(2)}, u32[]{:S(2)}) collective-permute-start(s32[4,8]{1,0:T(4,128)} %refs_0_.1), channel_id=1, source_target_pairs={{0,64},{32,96},{64,0},{96,32},{1,65},{33,97},{65,1},{97,33},{2,66}... | collective-permute-start | bytes 392 | tf_op jit(solution)/shard_map/ppermute | solution.py:585
  3.9 0.6 collective-permute-start
  4.5 2.6 %collective-permute-start.2 = (s32[4,8]{1,0:T(4,128)}, s32[4,8]{1,0:T(4,128)}, u32[]{:S(2)}, u32[]{:S(2)}) collective-permute-start(s32[4,8]{1,0:T(4,128)} %refs_0_.1), channel_id=1, source_target_pairs={{0,96},{32,0},{64,32},{96,64},{1,97},{33,1},{65,33},{97,65},{2,98}... | collective-permute-start | bytes 392 | tf_op jit(solution)/shard_map/ppermute | solution.py:585
  7.2 1.9 %collective-permute-done.refs_1_ = s32[4,8]{1,0:T(4,128)} collective-permute-done((s32[4,8]{1,0:T(4,128)}, s32[4,8]{1,0:T(4,128)}, u32[]{:S(2)}, u32[]{:S(2)}) %collective-permute-start) | collective-permute-done | bytes 160 | tf_op jit(solution)/shard_map/ppermute | solution.py:585
  9.0 2.4 %shard_map.95 = (bf16[4,560,128]{2,1,0:T(8,128)(2,1)}, f32[32,128]{1,0:T(8,128)}) custom-call(s32[1]{0:T(128)} %bitcast.place_ref, s32[4,8]{1,0:T(4,128)} %refs_0_.1, s32[4,8]{1,0:T(4,128)} %collective-permute-done.refs_1_, s32[4,8]{1,0:T(4,128)} %collective-permute-done.1.refs_2_, s32[4,8]{1,0:T(4,128)} %collective-permute-done.2.refs_3_, ...), custom_call_target="tpu_custom_call" | custom-call | tf_op jit(solution)/shard_map/pallas_call | solution.py:256
  11.4 4.5 %all-to-all-start = ((bf16[4,560,128]{2,1,0:T(8,128)(2,1)}), bf16[4,560,128]{2,1,0:T(8,128)(2,1)}, u32[]{:S(2)}, u32[]{:S(2)}) async-start(bf16[4,560,128]{2,1,0:T(8,128)(2,1)} %get-tuple-element.46), calls=%async_computation | async-start | bytes 1146880 | tf_op jit(solution)/shard_map/all_to_all | solution.py:623
  15.9 2.8 %shard_map.97.refs_0_ = s32[1048576]{0:T(1024)} custom-call(s32[1]{0:T(128)} %bitcast.6.half_ref.refs_4_, s32[8,64]{1,0:T(8,128)} %bitcast.62, s32[1,64]{1,0:T(1,128)} %bitcast.68, s32[8,64]{1,0:T(8,128)} %collective-permute-done.3.refs_2_, s32[1,64]{1,0:T(1,128)} %collective-permute-done.4.refs_3_), custom_call_target="tpu_custom_call" | custom-call | tf_op jit(solution)/shard_map/pallas_call | solution.py:196
  18.7 5.7 %shard_map.96.refs_0_ = s32[1048576]{0:T(1024)} custom-call(s32[1]{0:T(128)} %bitcast.6.half_ref.refs_4_, s32[8,64]{1,0:T(8,128)} %bitcast.63, s32[1,64]{1,0:T(1,128)} %bitcast.69, s32[8,64]{1,0:T(8,128)} %collective-permute-done.3.refs_2_, s32[1,64]{1,0:T(1,128)} %collective-permute-done.4.refs_3_), custom_call_target="tpu_custom_call" | custom-call | tf_op jit(solution)/shard_map/pallas_call | solution.py:196
  24.4 1.4 %all-to-all-done.refs_1_ = bf16[4,560,128]{2,1,0:T(8,128)(2,1)} async-done(((bf16[4,560,128]{2,1,0:T(8,128)(2,1)}), bf16[4,560,128]{2,1,0:T(8,128)(2,1)}, u32[]{:S(2)}, u32[]{:S(2)}) %all-to-all-start) | async-done | bytes 573472 | tf_op jit(solution)/shard_map/all_to_all | solution.py:623
  25.8 2.3 %collective-permute-done.5.refs_2_ = bf16[4,560,128]{2,1,0:T(8,128)(2,1)} collective-permute-done((bf16[4,560,128]{2,1,0:T(8,128)(2,1)}, bf16[4,560,128]{2,1,0:T(8,128)(2,1)}, u32[]{:S(2)}, u32[]{:S(2)}) %collective-permute-start.5) | collective-permute-done | bytes 573472 | tf_op jit(solution)/shard_map/ppermute | solution.py:585
  28.1 4.9 %shard_map.98 = (f32[16,32,128]{2,1,0:T(8,128)}, bf16[66,128,128]{2,1,0:T(8,128)(2,1)}) custom-call(s32[1048576]{0:T(1024)} %shard_map.96.refs_0_, bf16[4,560,128]{2,1,0:T(8,128)(2,1)} %all-to-all-done.refs_1_, bf16[4,560,128]{2,1,0:T(8,128)(2,1)} %collective-permute-done.5.refs_2_, bf16[64,8192]{1,0:T(8,128)(2,1)} %bitcast.58, s32[1]{0:T(128)} %bitcast.6.half_ref.refs_4_), custom_call_target="tpu_custom_call" | custom-call | tf_op jit(solution)/shard_map/pallas_call | solution.py:558
  33.0 9.6 %all-to-all-start.1 = ((f32[16,32,128]{2,1,0:T(8,128)}), f32[16,32,128]{2,1,0:T(8,128)S(1)}, u32[]{:S(2)}, u32[]{:S(2)}) async-start(f32[16,32,128]{2,1,0:T(8,128)} %get-tuple-element.69), calls=%async_computation.1 | async-start | bytes 524288 | tf_op jit(solution)/shard_map/all_to_all | solution.py:639
  42.6 0.7 copy-done
  43.4 0.7 copy-done.2
  44.1 3.4 %shard_map.99 = (bf16[2,33,128,128]{3,2,1,0:T(8,128)(2,1)}, f32[32,128]{1,0:T(8,128)S(1)}, bf16[128,128]{1,0:T(8,128)(2,1)S(1)}, s32[32]{0:T(128)S(1)}) custom-call(s32[1]{0:T(128)} %bitcast.6.half_ref.refs_4_, s32[1]{0:T(128)} %bitcast.place_ref, bf16[64,8192]{1,0:T(8,128)(2,1)} %bitcast.59, f32[64,128]{1,0:T(8,128)S(1)} %bitcast.57, s32[4,8]{1,0:T(4,128)S(1)} %copy-done.2, ...), custom_call_target="tpu_custom_call" | custom-call | tf_op jit(solution)/shard_map/pallas_call | solution.py:338
  47.4 4.8 %all-to-all-done.1.refs_4_ = f32[16,32,128]{2,1,0:T(8,128)S(1)} async-done(((f32[16,32,128]{2,1,0:T(8,128)}), f32[16,32,128]{2,1,0:T(8,128)S(1)}, u32[]{:S(2)}, u32[]{:S(2)}) %all-to-all-start.1) | async-done | bytes 262176 | tf_op jit(solution)/shard_map/all_to_all | solution.py:639
  52.2 3.7 %shard_map.100 = f32[1,64,128]{2,1,0:T(8,128)S(1)} custom-call(s32[1048576]{0:T(1024)} %shard_map.97.refs_0_, bf16[4,560,128]{2,1,0:T(8,128)(2,1)} %all-to-all-done.refs_1_, bf16[4,560,128]{2,1,0:T(8,128)(2,1)} %collective-permute-done.5.refs_2_, bf16[2,33,128,128]{3,2,1,0:T(8,128)(2,1)} %get-tuple-element.67.refs_3_.refs_2_, ...), custom_call_target="tpu_custom_call" | custom-call | tf_op jit(solution)/shard_map/pallas_call | solution.py:558
  55.9 0.1 collective-permute-start.6
  56.0 0.5 collective-permute-start.10
  56.5 0.7 collective-permute-done.6
  57.2 2.2 %collective-permute-start.9 = (f32[64,128]{1,0:T(8,128)S(1)}, f32[64,128]{1,0:T(8,128)S(1)}, u32[]{:S(2)}, u32[]{:S(2)}) collective-permute-start(f32[64,128]{1,0:T(8,128)S(1)} %multiply_add_fusion.1.refs_3_), channel_id=1, source_target_pairs={{0,96},{32,0},{64,32},{96,64},{1,97},{33,1},{65,33},{97,65},{2,98}... | collective-permute-start | bytes 98312 | tf_op jit(solution)/shard_map/ppermute | solution.py:585
  59.5 1.2 collective-permute-start.8
  60.7 0.7 collective-permute-start.7
  61.4 3.5 %collective-permute-done.8.refs_5_ = f32[64,128]{1,0:T(8,128)S(1)} collective-permute-done((f32[64,128]{1,0:T(8,128)S(1)}, f32[64,128]{1,0:T(8,128)S(1)}, u32[]{:S(2)}, u32[]{:S(2)}) %collective-permute-start.8) | collective-permute-done | bytes 32800 | tf_op jit(solution)/shard_map/ppermute | solution.py:585
  64.9 0.9 collective-permute-done.7.refs_4_
  65.8 3.8 %shard_map.101 = f32[16,32,128]{2,1,0:T(8,128)S(1)} custom-call(s32[1048576]{0:T(1024)} %shard_map.96.refs_0_, bf16[66,128,128]{2,1,0:T(8,128)(2,1)} %get-tuple-element.68.refs_1_, bf16[2,33,128,128]{3,2,1,0:T(8,128)(2,1)} %get-tuple-element.67.refs_3_.refs_2_, f32[64,128]{1,0:T(8,128)S(1)} %multiply_add_fusion.1.refs_3_, ...), custom_call_target="tpu_custom_call" | custom-call | tf_op jit(solution)/shard_map/pallas_call | solution.py:558
  69.6 14.6 %all_to_all.20.refs_4_ = f32[16,32,128]{2,1,0:T(8,128)S(1)} all-to-all(f32[16,32,128]{2,1,0:T(8,128)S(1)} %shard_map.101), channel_id=1, replica_groups={{0,2,4,6,8,10,12,14,16,18,20,22,24,26,28,30},{1,3,5,7,9,11,13,15,17,19,..., dimensions={0} | all-to-all | bytes 524288 | tf_op jit(solution)/shard_map/all_to_all | solution.py:639
  84.1 3.7 %shard_map.102 = f32[1,64,128]{2,1,0:T(8,128)S(1)} custom-call(s32[1048576]{0:T(1024)} %shard_map.97.refs_0_, bf16[4,560,128]{2,1,0:T(8,128)(2,1)} %all-to-all-done.refs_1_, bf16[4,560,128]{2,1,0:T(8,128)(2,1)} %collective-permute-done.5.refs_2_, bf16[2,33,128,128]{3,2,1,0:T(8,128)(2,1)} %get-tuple-element.67.refs_3_.refs_2_, ...), custom_call_target="tpu_custom_call" | custom-call | tf_op jit(solution)/shard_map/pallas_call | solution.py:558
  87.8 0.1 collective-permute-start.11
  87.9 1.2 collective-permute-done.11
  89.2 1.7 %collective-permute-start.14 = (f32[64,128]{1,0:T(8,128)S(1)}, f32[64,128]{1,0:T(8,128)S(1)}, u32[]{:S(2)}, u32[]{:S(2)}) collective-permute-start(f32[64,128]{1,0:T(8,128)S(1)} %multiply_add_fusion.refs_3_), channel_id=1, source_target_pairs={{0,96},{32,0},{64,32},{96,64},{1,97},{33,1},{65,33},{97,65},{2,98}... | collective-permute-start | bytes 98312 | tf_op jit(solution)/shard_map/ppermute | solution.py:585
  90.9 2.8 %collective-permute-start.13 = (f32[64,128]{1,0:T(8,128)S(1)}, f32[64,128]{1,0:T(8,128)S(1)}, u32[]{:S(2)}, u32[]{:S(2)}) collective-permute-start(f32[64,128]{1,0:T(8,128)S(1)} %multiply_add_fusion.refs_3_), channel_id=1, source_target_pairs={{0,64},{32,96},{64,0},{96,32},{1,65},{33,97},{65,1},{97,33},{2,66}... | collective-permute-start | bytes 98312 | tf_op jit(solution)/shard_map/ppermute | solution.py:585
  93.7 1.3 collective-permute-start.12
  95.0 1.6 %collective-permute-done.13.refs_5_ = f32[64,128]{1,0:T(8,128)S(1)} collective-permute-done((f32[64,128]{1,0:T(8,128)S(1)}, f32[64,128]{1,0:T(8,128)S(1)}, u32[]{:S(2)}, u32[]{:S(2)}) %collective-permute-start.13) | collective-permute-done | bytes 32800 | tf_op jit(solution)/shard_map/ppermute | solution.py:585
  96.6 2.2 %collective-permute-done.12.refs_4_ = f32[64,128]{1,0:T(8,128)S(1)} collective-permute-done((f32[64,128]{1,0:T(8,128)S(1)}, f32[64,128]{1,0:T(8,128)S(1)}, u32[]{:S(2)}, u32[]{:S(2)}) %collective-permute-start.12) | collective-permute-done | bytes 32800 | tf_op jit(solution)/shard_map/ppermute | solution.py:585
  98.8 3.8 %shard_map.103 = f32[16,32,128]{2,1,0:T(8,128)S(1)} custom-call(s32[1048576]{0:T(1024)} %shard_map.96.refs_0_, bf16[66,128,128]{2,1,0:T(8,128)(2,1)} %get-tuple-element.68.refs_1_, bf16[2,33,128,128]{3,2,1,0:T(8,128)(2,1)} %get-tuple-element.67.refs_3_.refs_2_, f32[64,128]{1,0:T(8,128)S(1)} %multiply_add_fusion.refs_3_, ...), custom_call_target="tpu_custom_call" | custom-call | tf_op jit(solution)/shard_map/pallas_call | solution.py:558
  102.6 15.0 %all_to_all.21.refs_4_ = f32[16,32,128]{2,1,0:T(8,128)S(1)} all-to-all(f32[16,32,128]{2,1,0:T(8,128)S(1)} %shard_map.103), channel_id=1, replica_groups={{0,2,4,6,8,10,12,14,16,18,20,22,24,26,28,30},{1,3,5,7,9,11,13,15,17,19,..., dimensions={0} | all-to-all | bytes 524288 | tf_op jit(solution)/shard_map/all_to_all | solution.py:639
  117.5 3.9 %shard_map.104 = (f32[1,64,128]{2,1,0:T(8,128)S(1)}, f32[32,128]{1,0:T(8,128)S(1)}) custom-call(s32[1048576]{0:T(1024)} %shard_map.97.refs_0_, bf16[4,560,128]{2,1,0:T(8,128)(2,1)} %all-to-all-done.refs_1_, bf16[4,560,128]{2,1,0:T(8,128)(2,1)} %collective-permute-done.5.refs_2_, bf16[2,33,128,128]{3,2,1,0:T(8,128)(2,1)} %get-tuple-element.67.refs_3_.refs_2_, ...), custom_call_target="tpu_custom_call" | custom-call | tf_op jit(solution)/shard_map/pallas_call | solution.py:558
  121.5 0.1 collective-permute-start.16
  121.6 0.5 collective-permute-start.15
  122.1 0.7 collective-permute-done.16
  122.8 0.8 collective-permute-start.19
  123.7 3.7 %collective-permute-start.18 = (f32[8,128]{1,0:T(8,128)S(1)}, f32[8,128]{1,0:T(8,128)S(1)}, u32[]{:S(2)}, u32[]{:S(2)}) collective-permute-start(f32[8,128]{1,0:T(8,128)S(1)} %get-tuple-element.89), channel_id=1, source_target_pairs={{0,64},{32,96},{64,0},{96,32},{1,65},{33,97},{65,1},{97,33},{2,66}... | collective-permute-start | bytes 12296 | tf_op jit(solution)/shard_map/ppermute | solution.py:661
  127.4 1.3 collective-permute-start.17
  128.7 0.6 maximum_bitcast_fusion
  129.4 2.9 %collective-permute-done.17.refs_1_ = f32[8,128]{1,0:T(8,128)S(1)} collective-permute-done((f32[8,128]{1,0:T(8,128)S(1)}, f32[8,128]{1,0:T(8,128)S(1)}, u32[]{:S(2)}, u32[]{:S(2)}) %collective-permute-start.17) | collective-permute-done | bytes 4128 | tf_op jit(solution)/shard_map/ppermute | solution.py:661
  132.2 1.2 shard_map.105
  (25 shorter events, 0.2 us)
Async XLA Ops:
  0.6 8.4 %collective-permute-start.3 = (s32[8,64]{1,0:T(8,128)}, s32[8,64]{1,0:T(8,128)}, u32[]{:S(2)}, u32[]{:S(2)}) collective-permute-start(s32[8,64]{1,0:T(8,128)} %bitcast.61), channel_id=1, source_target_pairs={{0,1},{1,0},{2,3},{3,2},{4,5},{5,4},{6,7},{7,6},{8,9},{9,8},{10,11... | collective-permute-start | bytes 6152 | tf_op jit(solution)/shard_map/ppermute | solution.py:585
  0.7 6.4 %collective-permute-start.1 = (s32[4,8]{1,0:T(4,128)}, s32[4,8]{1,0:T(4,128)}, u32[]{:S(2)}, u32[]{:S(2)}) collective-permute-start(s32[4,8]{1,0:T(4,128)} %refs_0_.1), channel_id=1, source_target_pairs={{0,64},{32,96},{64,0},{96,32},{1,65},{33,97},{65,1},{97,33},{2,66}... | collective-permute-start | bytes 392 | tf_op jit(solution)/shard_map/ppermute | solution.py:585
  3.9 5.1 %collective-permute-start = (s32[4,8]{1,0:T(4,128)}, s32[4,8]{1,0:T(4,128)}, u32[]{:S(2)}, u32[]{:S(2)}) collective-permute-start(s32[4,8]{1,0:T(4,128)} %refs_0_.1), channel_id=1, source_target_pairs={{0,32},{32,64},{64,96},{96,0},{1,33},{33,65},{65,97},{97,1},{2,34}... | collective-permute-start | bytes 392 | tf_op jit(solution)/shard_map/ppermute | solution.py:585
  4.5 4.5 %collective-permute-start.2 = (s32[4,8]{1,0:T(4,128)}, s32[4,8]{1,0:T(4,128)}, u32[]{:S(2)}, u32[]{:S(2)}) collective-permute-start(s32[4,8]{1,0:T(4,128)} %refs_0_.1), channel_id=1, source_target_pairs={{0,96},{32,0},{64,32},{96,64},{1,97},{33,1},{65,33},{97,65},{2,98}... | collective-permute-start | bytes 392 | tf_op jit(solution)/shard_map/ppermute | solution.py:585
  7.2 1.9 %collective-permute-start.4 = (s32[1,64]{1,0:T(1,128)}, s32[1,64]{1,0:T(1,128)}, u32[]{:S(2)}, u32[]{:S(2)}) collective-permute-start(s32[1,64]{1,0:T(1,128)} %bitcast.67), channel_id=1, source_target_pairs={{0,1},{1,0},{2,3},{3,2},{4,5},{5,4},{6,7},{7,6},{8,9},{9,8},{10,11... | collective-permute-start | bytes 776 | tf_op jit(solution)/shard_map/ppermute | solution.py:585
  11.4 14.4 %all-to-all-start = ((bf16[4,560,128]{2,1,0:T(8,128)(2,1)}), bf16[4,560,128]{2,1,0:T(8,128)(2,1)}, u32[]{:S(2)}, u32[]{:S(2)}) async-start(bf16[4,560,128]{2,1,0:T(8,128)(2,1)} %get-tuple-element.46), calls=%async_computation | async-start | bytes 1146880 | tf_op jit(solution)/shard_map/all_to_all | solution.py:623
  25.8 2.3 %collective-permute-start.5 = (bf16[4,560,128]{2,1,0:T(8,128)(2,1)}, bf16[4,560,128]{2,1,0:T(8,128)(2,1)}, u32[]{:S(2)}, u32[]{:S(2)}) collective-permute-start(bf16[4,560,128]{2,1,0:T(8,128)(2,1)} %all-to-all-done.refs_1_), channel_id=1, source_target_pairs={{0,1},{1,0},{2,3},{3,2},{4,5},{5,4},{6,7},{7,6},{8,9},{9,8},{10,11... | collective-permute-start | bytes 1720328 | tf_op jit(solution)/shard_map/ppermute | solution.py:585
  33.0 19.1 %all-to-all-start.1 = ((f32[16,32,128]{2,1,0:T(8,128)}), f32[16,32,128]{2,1,0:T(8,128)S(1)}, u32[]{:S(2)}, u32[]{:S(2)}) async-start(f32[16,32,128]{2,1,0:T(8,128)} %get-tuple-element.69), calls=%async_computation.1 | async-start | bytes 524288 | tf_op jit(solution)/shard_map/all_to_all | solution.py:639
  42.6 0.8 copy-start
  43.4 0.7 copy-start.2
  55.9 1.3 collective-permute-start.6
  56.0 5.4 %collective-permute-start.10 = (bf16[128,128]{1,0:T(8,128)(2,1)S(1)}, bf16[128,128]{1,0:T(8,128)(2,1)S(1)}, u32[]{:S(2)}, u32[]{:S(2)}) collective-permute-start(bf16[128,128]{1,0:T(8,128)(2,1)S(1)} %get-tuple-element.70.refs_7_), channel_id=1, source_target_pairs={{0,1},{1,0},{2,3},{3,2},{4,5},{5,4},{6,7},{7,6},{8,9},{9,8},{10,11... | collective-permute-start | bytes 98312 | tf_op jit(solution)/shard_map/ppermute | solution.py:585
  57.2 4.2 %collective-permute-start.9 = (f32[64,128]{1,0:T(8,128)S(1)}, f32[64,128]{1,0:T(8,128)S(1)}, u32[]{:S(2)}, u32[]{:S(2)}) collective-permute-start(f32[64,128]{1,0:T(8,128)S(1)} %multiply_add_fusion.1.refs_3_), channel_id=1, source_target_pairs={{0,96},{32,0},{64,32},{96,64},{1,97},{33,1},{65,33},{97,65},{2,98}... | collective-permute-start | bytes 98312 | tf_op jit(solution)/shard_map/ppermute | solution.py:585
  59.5 5.4 %collective-permute-start.8 = (f32[64,128]{1,0:T(8,128)S(1)}, f32[64,128]{1,0:T(8,128)S(1)}, u32[]{:S(2)}, u32[]{:S(2)}) collective-permute-start(f32[64,128]{1,0:T(8,128)S(1)} %multiply_add_fusion.1.refs_3_), channel_id=1, source_target_pairs={{0,64},{32,96},{64,0},{96,32},{1,65},{33,97},{65,1},{97,33},{2,66}... | collective-permute-start | bytes 98312 | tf_op jit(solution)/shard_map/ppermute | solution.py:585
  60.7 5.1 %collective-permute-start.7 = (f32[64,128]{1,0:T(8,128)S(1)}, f32[64,128]{1,0:T(8,128)S(1)}, u32[]{:S(2)}, u32[]{:S(2)}) collective-permute-start(f32[64,128]{1,0:T(8,128)S(1)} %multiply_add_fusion.1.refs_3_), channel_id=1, source_target_pairs={{0,32},{32,64},{64,96},{96,0},{1,33},{33,65},{65,97},{97,1},{2,34}... | collective-permute-start | bytes 98312 | tf_op jit(solution)/shard_map/ppermute | solution.py:585
  87.8 1.3 collective-permute-start.11
  89.2 5.8 %collective-permute-start.14 = (f32[64,128]{1,0:T(8,128)S(1)}, f32[64,128]{1,0:T(8,128)S(1)}, u32[]{:S(2)}, u32[]{:S(2)}) collective-permute-start(f32[64,128]{1,0:T(8,128)S(1)} %multiply_add_fusion.refs_3_), channel_id=1, source_target_pairs={{0,96},{32,0},{64,32},{96,64},{1,97},{33,1},{65,33},{97,65},{2,98}... | collective-permute-start | bytes 98312 | tf_op jit(solution)/shard_map/ppermute | solution.py:585
  90.9 5.7 %collective-permute-start.13 = (f32[64,128]{1,0:T(8,128)S(1)}, f32[64,128]{1,0:T(8,128)S(1)}, u32[]{:S(2)}, u32[]{:S(2)}) collective-permute-start(f32[64,128]{1,0:T(8,128)S(1)} %multiply_add_fusion.refs_3_), channel_id=1, source_target_pairs={{0,64},{32,96},{64,0},{96,32},{1,65},{33,97},{65,1},{97,33},{2,66}... | collective-permute-start | bytes 98312 | tf_op jit(solution)/shard_map/ppermute | solution.py:585
  93.7 5.1 %collective-permute-start.12 = (f32[64,128]{1,0:T(8,128)S(1)}, f32[64,128]{1,0:T(8,128)S(1)}, u32[]{:S(2)}, u32[]{:S(2)}) collective-permute-start(f32[64,128]{1,0:T(8,128)S(1)} %multiply_add_fusion.refs_3_), channel_id=1, source_target_pairs={{0,32},{32,64},{64,96},{96,0},{1,33},{33,65},{65,97},{97,1},{2,34}... | collective-permute-start | bytes 98312 | tf_op jit(solution)/shard_map/ppermute | solution.py:585
  117.5 14.7 %copy-start.1 = (f32[32,128]{1,0:T(8,128)S(1)}, f32[32,128]{1,0:T(8,128)}, u32[]{:S(2)}) copy-start(f32[32,128]{1,0:T(8,128)} %get-tuple-element.81.refs_4_) | copy-start | bytes 49156
  121.5 1.3 collective-permute-start.16
  121.6 7.1 %collective-permute-start.15 = (f32[32,128]{1,0:T(8,128)S(1)}, f32[32,128]{1,0:T(8,128)S(1)}, u32[]{:S(2)}, u32[]{:S(2)}) collective-permute-start(f32[32,128]{1,0:T(8,128)S(1)} %multiply_add_fusion.2), channel_id=1, source_target_pairs={{0,1},{1,0},{2,3},{3,2},{4,5},{5,4},{6,7},{7,6},{8,9},{9,8},{10,11... | collective-permute-start | bytes 49160 | tf_op jit(solution)/shard_map/ppermute | solution.py:585
  122.8 6.5 %collective-permute-start.19 = (f32[8,128]{1,0:T(8,128)S(1)}, f32[8,128]{1,0:T(8,128)S(1)}, u32[]{:S(2)}, u32[]{:S(2)}) collective-permute-start(f32[8,128]{1,0:T(8,128)S(1)} %get-tuple-element.88), channel_id=1, source_target_pairs={{0,96},{32,0},{64,32},{96,64},{1,97},{33,1},{65,33},{97,65},{2,98}... | collective-permute-start | bytes 12296 | tf_op jit(solution)/shard_map/ppermute | solution.py:661
  123.7 5.7 %collective-permute-start.18 = (f32[8,128]{1,0:T(8,128)S(1)}, f32[8,128]{1,0:T(8,128)S(1)}, u32[]{:S(2)}, u32[]{:S(2)}) collective-permute-start(f32[8,128]{1,0:T(8,128)S(1)} %get-tuple-element.89), channel_id=1, source_target_pairs={{0,64},{32,96},{64,0},{96,32},{1,65},{33,97},{65,1},{97,33},{2,66}... | collective-permute-start | bytes 12296 | tf_op jit(solution)/shard_map/ppermute | solution.py:661
  127.4 4.8 %collective-permute-start.17 = (f32[8,128]{1,0:T(8,128)S(1)}, f32[8,128]{1,0:T(8,128)S(1)}, u32[]{:S(2)}, u32[]{:S(2)}) collective-permute-start(f32[8,128]{1,0:T(8,128)S(1)} %get-tuple-element.90), channel_id=1, source_target_pairs={{0,32},{32,64},{64,96},{96,0},{1,33},{33,65},{65,97},{97,1},{2,34}... | collective-permute-start | bytes 12296 | tf_op jit(solution)/shard_map/ppermute | solution.py:661
